TPU v7x, 128 devices: a whole 4x4x4 slice. The times are simulated.
128 devices in a mesh: section: 4 (over z_lo, core), dp: 16 (over x, y), tensor: 2 (over z_hi).
Axes of the slice: x: 4, y: 4, z: 4 (z_hi: 2, z_lo: 2; z = z_hi * 2 + z_lo), core: 2. Of those that a mesh axis runs over, the one named last changes fastest.
Arguments:
- layer_inputs: bfloat16 [4, 2, 2048, 8192], P('section', None, 'dp'), may hold values from -6 to 6
- value_cotangent: bfloat16 [4, 2, 2048, 1024], P('section', None, 'dp', 'tensor'), may hold values from -6 to 6
- value_weight: bfloat16 [4, 8192, 1024], P('section', 'dp', 'tensor'), may hold values from -0.0625 to 0.0625
- norm_gain: float32 [4, 8192], P('section'), may hold values from 0.25 to 1.75
- skip_keep: int32 [4, 2, 16], P('section', None, 'dp'), may hold values from 0 to 1, as said below
- top_grad: bfloat16 [2, 2048, 8192], P(None, 'dp', 'tensor'), may hold values from -6 to 6
Outputs:
- section_grads: float32 [4, 2, 2048, 8192], P('section', None, 'dp', 'tensor')
- weight_grad: float32 [4, 8192, 1024], P('section', 'dp', 'tensor')
Inputs may be any that keep to these rules, and one draw needn't show every extreme that they name: `skip_keep`: 1 keeps a block of 128 consecutive rows in a layer, 0 lets it bypass the layer.
All inputs are finite; a program needn't handle non-finite values.
Results may differ from a plain program's by a relative error of at most 0.0029.
Values may be sent and summed in bfloat16 or wider, within the bound.
A program may use at most 128 MiB of HBM per device.

v0:
```python
import jax
import jax.numpy as jnp
from jax import lax
from jax.sharding import PartitionSpec as P

EPSILON = 1e-05


def from_behind(value, axis, steps):
    count = lax.axis_size(axis)
    first, last = (max(0, -steps), min(count, count - steps))
    return lax.ppermute(value, axis, [(source, source + steps) for source in range(first, last)])


def branch_part(inputs, cotangent, weight, gain):
    model_width = inputs.shape[1]
    half_width = model_width // lax.axis_size("tensor")
    offset = lax.axis_index("tensor") * half_width
    inputs_f = inputs.astype(jnp.float32)
    inverse = lax.rsqrt(jnp.mean(inputs_f * inputs_f, axis=-1, keepdims=True) + EPSILON)
    partial_value = lax.dot_general(
        cotangent, weight, (((1,), (1,)), ((), ())), preferred_element_type=jnp.float32
    )
    normed_grad = lax.psum(partial_value, "tensor")
    scaled = gain * normed_grad
    row_dot = jnp.sum(inputs_f * scaled, axis=-1, keepdims=True)
    branch = inverse * scaled - inputs_f * inverse**3 * row_dot / model_width
    return lax.dynamic_slice_in_dim(branch, offset, half_width, 1)


def on_device(layer_inputs, value_cotangent, value_weight, norm_gain, skip_keep, top_grad):
    sections = lax.axis_size("section")
    position = lax.axis_index("section")
    layers_here, batches, row_count, model_width = layer_inputs.shape
    block_rows = row_count // skip_keep.shape[2]
    weights = lax.all_gather(value_weight, "dp", axis=1, tiled=True)
    layer_no = 0
    per_batch = []
    for batch_no in range(batches):
        keep_rows = jnp.repeat(skip_keep[layer_no, batch_no].astype(jnp.float32), block_rows)[
            :, None
        ]
        branch = branch_part(
            layer_inputs[layer_no, batch_no],
            value_cotangent[layer_no, batch_no],
            weights[layer_no],
            norm_gain[layer_no],
        )
        per_batch.append(keep_rows * branch)
    branches = [jnp.stack(per_batch)]
    inbound = jnp.zeros(top_grad.shape[1:], jnp.float32)
    results = jnp.zeros(top_grad.shape, jnp.float32)
    for moment in range(sections + batches - 1):
        micro_no = moment - (sections - 1 - position)
        active = (micro_no >= 0) & (micro_no < batches)
        picked = jnp.clip(micro_no, 0, batches - 1)
        running = jnp.where(
            position == sections - 1,
            lax.dynamic_index_in_dim(top_grad, picked, 0, keepdims=False).astype(jnp.float32),
            inbound,
        )
        for layer_no in reversed(range(layers_here)):
            added = lax.dynamic_index_in_dim(branches[layer_no], picked, 0, keepdims=False)
            running = running + added
        previous = lax.dynamic_index_in_dim(results, picked, 0, keepdims=False)
        results = lax.dynamic_update_index_in_dim(
            results, jnp.where(active, running, previous), picked, 0
        )
        if moment < sections + batches - 2:
            inbound = from_behind(running, "section", -1)
    total_rows = batches * row_count * lax.axis_size("dp")
    factor = float(total_rows) ** (-0.5)
    layer_no = 0
    inputs_f = layer_inputs[layer_no].astype(jnp.float32)
    inverse = lax.rsqrt(jnp.mean(inputs_f * inputs_f, axis=-1, keepdims=True) + EPSILON)
    normed = (
        (inputs_f * inverse * norm_gain[layer_no])
        .astype(jnp.bfloat16)
        .reshape(batches * row_count, model_width)
    )
    keep_rows = jnp.repeat(skip_keep[layer_no].astype(jnp.float32), block_rows, axis=1)[..., None]
    masked = (value_cotangent[layer_no].astype(jnp.float32) * keep_rows).astype(jnp.bfloat16)
    masked = masked.reshape(batches * row_count, masked.shape[-1])
    summed = lax.psum_scatter(
        lax.dot_general(
            normed, masked, (((0,), (0,)), ((), ())), preferred_element_type=jnp.float32
        ),
        "dp",
        scatter_dimension=0,
        tiled=True,
    )
    grads_out = [summed * factor]
    return (results[None], jnp.stack(grads_out))


def solution(mesh):
    placed = (
        P("section", None, "dp", None),
        P("section", None, "dp", "tensor"),
        P("section", "dp", "tensor"),
        P("section", None),
        P("section", None, "dp"),
        P(None, "dp", "tensor"),
    )
    return jax.shard_map(
        on_device,
        mesh=mesh,
        in_specs=placed,
        out_specs=(P("section", None, "dp", "tensor"), P("section", "dp", "tensor")),
        check_vma=False,
    )
```

profile of v0, /device:TPU:1, one launch (start us, length us, event | category | flops | bytes accessed | tf_op | source)
XLA Modules:
  0.0 456.1 jit_solution(5508298958464215754)
XLA Ops:
  8.0 76.0 %all-gather.2.cloned.1.call-done = bf16[1,8192,512]{2,1,0:T(8,128)(2,1)} async-done(((bf16[1,512,512]{2,1,0:T(8,128)(2,1)}), bf16[1,8192,512]{2,1,0:T(8,128)(2,1)}) %all-gather.2.cloned.1.call-update) | async-done | bytes 8388624 | tf_op jit(solution)/shard_map/all_gather | solution.py:36
  84.0 8.4 %fusion.3 = f32[128,8192]{1,0:T(8,128)} fusion(bf16[1,8192,512]{2,1,0:T(8,128)(2,1)} %all-gather.2.cloned.1.call-done, bf16[1,2,128,512]{3,2,1,0:T(8,128)(2,1)} %param.7), kind=kOutput, calls=%fused_computation.6 | convolution fusion | flops 1073741824 | bytes 12713984 | tf_op jit(solution)/shard_map/dot_general | solution.py:21
  92.4 4.8 %fusion.5 = f32[128,8192]{1,0:T(8,128)} fusion(bf16[1,8192,512]{2,1,0:T(8,128)(2,1)S(1)} %copy-done.8, bf16[1,2,128,512]{3,2,1,0:T(8,128)(2,1)S(1)} %copy-done.16), kind=kOutput, calls=%fused_computation.8 | convolution fusion | flops 1073741824 | bytes 12713984 | tf_op jit(solution)/shard_map/dot_general | solution.py:21
  97.9 3.3 fusion
  101.3 9.0 %convolution_bitcast_fusion = f32[8192,512]{1,0:T(8,128)} fusion(bf16[1,2,128,8192]{3,2,1,0:T(8,128)(2,1)S(1)} %copy-done.5, f32[8192]{0:T(1024)S(1)} %bitcast.108, f32[2,128]{1,0:T(2,128)S(1)} %add_rsqrt_fusion, bf16[1,2,128,512]{3,2,1,0:T(8,128)(2,1)S(1)} %copy-done.16, f32[2]{0:T(128)S(1)} %convert_bitcast_fusion), kind=kOutput, calls=%fused_computation | convolution fusion | flops 2156265472 | bytes 21267464 | tf_op jit(solution)/shard_map/dot_general | solution.py:85
  112.3 6.7 %bitcast_convert_fusion.1 = (f32[128,8192]{1,0:T(8,128)}, f32[128,8192]{1,0:T(8,128)}) fusion(bf16[1,2,128,8192]{3,2,1,0:T(8,128)(2,1)} %param.6), kind=kLoop, calls=%fused_computation.69 | loop fusion | flops 2097152 | bytes 12582912 | tf_op jit(solution)/shard_map/convert_element_type | solution.py:19
  119.0 184.5 %all-reduce.3.cloned.1.call-done = (f32[128,8192]{1,0:T(8,128)}, f32[128,8192]{1,0:T(8,128)}) async-done(((f32[128,8192]{1,0:T(8,128)}, f32[128,8192]{1,0:T(8,128)}), (f32[128,8192]{1,0:T(8,128)}, f32[128,8192]{1,0:T(8,128)})) %all-reduce.3.cloned.1.call-update) | async-done | bytes 8388624 | tf_op jit(solution)/shard_map/psum | solution.py:24
  303.5 6.2 %multiply_reduce_fusion.2 = (f32[128]{0:T(128)S(1)}, f32[128]{0:T(128)S(1)}, f32[128]{0:T(128)S(1)}, f32[128]{0:T(128)S(1)}, f32[128,8192]{1,0:T(8,128)S(1)}, /*index=5*/f32[128,8192]{1,0:T(8,128)S(1)}) fusion(bf16[1,2,128,8192]{3,2,1,0:T(8,128)(2,1)} %param.6, f32[128,8192]{1,0:T(8,128)} %get-tuple-element.7, f32[8192]{0:T(1024)S(1)} %bitcast.109, ...), kind=kLoop, calls=%fused_computation.25 | loop fusion | flops 12582400 | bytes 21006336 | tf_op jit(solution)/shard_map/reduce_sum | solution.py:26
  314.4 2.0 fusion.45
  316.4 1.9 copy-done.6
  318.3 2.8 collective-permute-start
  321.1 1.9 constant_dynamic-slice_fusion.2
  323.0 23.2 %collective-permute-done = f32[128,4096]{1,0:T(8,128)} collective-permute-done((f32[128,4096]{1,0:T(8,128)}, f32[128,4096]{1,0:T(8,128)}, u32[]{:S(2)}, u32[]{:S(2)}) %collective-permute-start) | collective-permute-done | bytes 2097184 | tf_op jit(solution)/shard_map/ppermute | solution.py:12
  346.2 4.5 bitcast_dynamic-update-slice_fusion.2
  352.7 2.2 constant_dynamic-slice_fusion.1
  354.9 23.8 %collective-permute-done.1 = f32[128,4096]{1,0:T(8,128)} collective-permute-done((f32[128,4096]{1,0:T(8,128)}, f32[128,4096]{1,0:T(8,128)}, u32[]{:S(2)}, u32[]{:S(2)}) %collective-permute-start.1) | collective-permute-done | bytes 2097184 | tf_op jit(solution)/shard_map/ppermute | solution.py:12
  378.7 4.5 bitcast_dynamic-update-slice_fusion.1
  385.2 2.0 constant_dynamic-slice_fusion
  387.2 24.0 %collective-permute-done.2 = f32[128,4096]{1,0:T(8,128)} collective-permute-done((f32[128,4096]{1,0:T(8,128)}, f32[128,4096]{1,0:T(8,128)}, u32[]{:S(2)}, u32[]{:S(2)}) %collective-permute-start.2) | collective-permute-done | bytes 2097184 | tf_op jit(solution)/shard_map/ppermute | solution.py:12
  411.2 4.6 %bitcast_dynamic-update-slice_fusion = (f32[2,128,4096]{2,1,0:T(8,128)}, f32[128,4096]{1,0:T(8,128)}) fusion(f32[2,128,4096]{2,1,0:T(8,128)} %get-tuple-element.10, s32[]{:T(128)S(6)} %min.19, f32[1,128,4096]{2,1,0:T(8,128)S(1)} %constant_dynamic-slice_fusion, pred[]{:T(512)S(6)} %and.20, f32[1,128,4096]{2,1,0:T(8,128)S(1)} %get-tuple-element.26, ...), kind=kLoop, calls=%fused_computation.62 | loop fusion | flops 2621440 | bytes 13631494 | tf_op jit(solution)/shard_map/jit(dynamic_update_index_in_dim)/dynamic_update_slice | solution.py:66
  417.8 4.9 %copy.16 = f32[1,2,128,4096]{3,2,1,0:T(8,128)} copy(f32[1,2,128,4096]{3,2,1,0:T(8,128)} %bitcast.107) | data formatting | bytes 8388608
  422.7 20.8 %collective-permute-done.3 = f32[128,4096]{1,0:T(8,128)} collective-permute-done((f32[128,4096]{1,0:T(8,128)}, f32[128,4096]{1,0:T(8,128)}, u32[]{:S(2)}, u32[]{:S(2)}) %collective-permute-start.3) | collective-permute-done | bytes 2097184 | tf_op jit(solution)/shard_map/ppermute | solution.py:12
  443.5 3.7 fusion.16
  447.2 2.3 multiply_bitcast_fusion
  (54 shorter events, 12.7 us)
Async XLA Ops:
  7.2 76.8 %all-gather.2.cloned.1.call-start = ((), (), s32[]{:S(2)}) async-start(), calls=%async_computation.1 | async-start | bytes 8912896 | tf_op jit(solution)/shard_map/all_gather | solution.py:36
  7.9 84.5 %copy-start.16 = (bf16[1,2,128,512]{3,2,1,0:T(8,128)(2,1)S(1)}, bf16[1,2,128,512]{3,2,1,0:T(8,128)(2,1)}, u32[]{:S(2)}) copy-start(bf16[1,2,128,512]{3,2,1,0:T(8,128)(2,1)} %param.7) | copy-start | bytes 786436
  7.9 295.6 %all-reduce.3.cloned.1.call-start = ((), (), s32[]{:S(2)}) async-start(), calls=%async_computation.3 | async-start | bytes 16777216 | tf_op jit(solution)/shard_map/psum | solution.py:24
  84.0 8.4 %copy-start.8 = (bf16[1,8192,512]{2,1,0:T(8,128)(2,1)S(1)}, bf16[1,8192,512]{2,1,0:T(8,128)(2,1)}, u32[]{:S(2)}) copy-start(bf16[1,8192,512]{2,1,0:T(8,128)(2,1)} %all-gather.2.cloned.1.call-done) | copy-start | bytes 25165828
  97.2 3.9 copy-start.17
  97.3 350.0 %reduce-scatter.2.cloned.1.call-start = ((), (), s32[]{:S(2)}) async-start(), calls=%async_computation.2 | async-start | bytes 17825792 | tf_op jit(solution)/shard_map/reduce_scatter | solution.py:84
  97.9 3.5 copy-start.5
  303.5 6.2 %copy-start.14 = (f32[128,8192]{1,0:T(8,128)S(1)}, f32[128,8192]{1,0:T(8,128)}, u32[]{:S(2)}) copy-start(f32[128,8192]{1,0:T(8,128)} %get-tuple-element.18) | copy-start | bytes 12582916
  303.5 7.1 %copy-start.15 = (f32[128,8192]{1,0:T(8,128)S(1)}, f32[128,8192]{1,0:T(8,128)}, u32[]{:S(2)}) copy-start(f32[128,8192]{1,0:T(8,128)} %get-tuple-element.19) | copy-start | bytes 12582916
  312.0 2.4 copy-start.9
  316.3 1.9 copy-start.6
  318.3 28.0 %collective-permute-start = (f32[128,4096]{1,0:T(8,128)}, f32[128,4096]{1,0:T(8,128)}, u32[]{:S(2)}, u32[]{:S(2)}) collective-permute-start(f32[128,4096]{1,0:T(8,128)} %get-tuple-element.16), channel_id=1, source_target_pairs={{32,0},{64,32},{96,64},{33,1},{65,33},{97,65},{34,2},{66,34},{98,6... | collective-permute-start | bytes 6291464 | tf_op jit(solution)/shard_map/ppermute | solution.py:12
  321.1 25.2 %copy-start.1 = (f32[1,128,4096]{2,1,0:T(8,128)S(1)}, f32[1,128,4096]{2,1,0:T(8,128)}, u32[]{:S(2)}) copy-start(f32[1,128,4096]{2,1,0:T(8,128)} %copy-done) | copy-start | bytes 6291460
  321.1 25.2 %copy-start.10 = (bf16[2,128,4096]{2,1,0:T(8,128)(2,1)S(1)}, bf16[2,128,4096]{2,1,0:T(8,128)(2,1)}, u32[]{:S(2)}) copy-start(bf16[2,128,4096]{2,1,0:T(8,128)(2,1)} %param.11) | copy-start | bytes 6291460
  350.8 28.0 %collective-permute-start.1 = (f32[128,4096]{1,0:T(8,128)}, f32[128,4096]{1,0:T(8,128)}, u32[]{:S(2)}, u32[]{:S(2)}) collective-permute-start(f32[128,4096]{1,0:T(8,128)} %get-tuple-element.13), channel_id=1, source_target_pairs={{32,0},{64,32},{96,64},{33,1},{65,33},{97,65},{34,2},{66,34},{98,6... | collective-permute-start | bytes 6291464 | tf_op jit(solution)/shard_map/ppermute | solution.py:12
  352.7 26.0 %copy-start.2 = (f32[1,128,4096]{2,1,0:T(8,128)S(1)}, f32[1,128,4096]{2,1,0:T(8,128)}, u32[]{:S(2)}) copy-start(f32[1,128,4096]{2,1,0:T(8,128)} %copy-done) | copy-start | bytes 6291460
  352.7 26.0 %copy-start.11 = (bf16[2,128,4096]{2,1,0:T(8,128)(2,1)S(1)}, bf16[2,128,4096]{2,1,0:T(8,128)(2,1)}, u32[]{:S(2)}) copy-start(bf16[2,128,4096]{2,1,0:T(8,128)(2,1)} %param.11) | copy-start | bytes 6291460
  383.3 28.0 %collective-permute-start.2 = (f32[128,4096]{1,0:T(8,128)}, f32[128,4096]{1,0:T(8,128)}, u32[]{:S(2)}, u32[]{:S(2)}) collective-permute-start(f32[128,4096]{1,0:T(8,128)} %get-tuple-element.11), channel_id=1, source_target_pairs={{32,0},{64,32},{96,64},{33,1},{65,33},{97,65},{34,2},{66,34},{98,6... | collective-permute-start | bytes 6291464 | tf_op jit(solution)/shard_map/ppermute | solution.py:12
  385.2 26.0 %copy-start.3 = (f32[1,128,4096]{2,1,0:T(8,128)S(1)}, f32[1,128,4096]{2,1,0:T(8,128)}, u32[]{:S(2)}) copy-start(f32[1,128,4096]{2,1,0:T(8,128)} %copy-done) | copy-start | bytes 6291460
  385.2 26.0 %copy-start.12 = (bf16[2,128,4096]{2,1,0:T(8,128)(2,1)S(1)}, bf16[2,128,4096]{2,1,0:T(8,128)(2,1)}, u32[]{:S(2)}) copy-start(bf16[2,128,4096]{2,1,0:T(8,128)(2,1)} %param.11) | copy-start | bytes 6291460
  415.8 27.7 %collective-permute-start.3 = (f32[128,4096]{1,0:T(8,128)}, f32[128,4096]{1,0:T(8,128)}, u32[]{:S(2)}, u32[]{:S(2)}) collective-permute-start(f32[128,4096]{1,0:T(8,128)} %get-tuple-element.9), channel_id=1, source_target_pairs={{32,0},{64,32},{96,64},{33,1},{65,33},{97,65},{34,2},{66,34},{98,6... | collective-permute-start | bytes 6291464 | tf_op jit(solution)/shard_map/ppermute | solution.py:12
  417.8 25.7 %copy-start.4 = (f32[1,128,4096]{2,1,0:T(8,128)S(1)}, f32[1,128,4096]{2,1,0:T(8,128)}, u32[]{:S(2)}) copy-start(f32[1,128,4096]{2,1,0:T(8,128)} %copy-done) | copy-start | bytes 6291460
  417.8 25.7 %copy-start.7 = (f32[2,128,4096]{2,1,0:T(8,128)S(1)}, f32[2,128,4096]{2,1,0:T(8,128)}, u32[]{:S(2)}) copy-start(f32[2,128,4096]{2,1,0:T(8,128)} %get-tuple-element.8) | copy-start | bytes 12582916
  417.8 25.7 %copy-start.13 = (bf16[2,128,4096]{2,1,0:T(8,128)(2,1)S(1)}, bf16[2,128,4096]{2,1,0:T(8,128)(2,1)}, u32[]{:S(2)}) copy-start(bf16[2,128,4096]{2,1,0:T(8,128)(2,1)} %param.11) | copy-start | bytes 6291460
  (2 other events, 2.0 us)
Sparse Core Ops, SparseCore 0:
  10.1 73.8 all-gather.1
  97.4 206.0 all-reduce.2
  306.9 109.6 reduce-scatter.1
where the time goes:
time: 457 us; the launch traced here: 456 us
  waiting for transfers between devices  353 us (77%)
  other arithmetic  39.2 us (9%)
  matrix products  22.3 us (5%)
  local copies, waits for them, and re-layouts  17.6 us (4%)
  between operations  15.3 us (3%)
  starting transfers between devices  8.62 us (2%)
    psum x1, waiting for transfers between devices, branch_part(): normed_grad = lax.psum(partial_value, 'tensor')  185 us
    ppermute x4, waiting for transfers between devices, from_behind(): lax.ppermute(value, axis, [(source, source + steps) for source in range(f...  91.8 us
    all_gather x1, waiting for transfers between devices, on_device(): weights = lax.all_gather(value_weight, 'dp', axis=1, tiled=True)  76 us
    dynamic_update_slice x4, other arithmetic, on_device(): lax.dynamic_update_index_in_dim(results, jnp.where(active, running, previ...  17.4 us
    dot_general x2, matrix products, branch_part(): lax.dot_general(cotangent, weight, (((1,), (1,)), ((), ())), preferred_el...  13.2 us
    unnamed x39, local copies, waits for them, and re-layouts  10.5 us
  transfers between devices with their start and end apart: 7, of which 6 were waited for; matrix products, arithmetic and copies ran while one was open for 13% of the time, Pallas kernels for 0%

commit v1 on v0

v1 whole, which is shorter than its diff:
```python
import functools

import jax
import jax.numpy as jnp
from jax import lax
from jax.experimental import pallas as pl
from jax.experimental.pallas import tpu as pltpu
from jax.sharding import PartitionSpec as P

EPSILON = 1e-05
MESH = pl.DeviceIdType.MESH
MB = 2
ROWS = 128
D = 8192
SUB = 1024
HALF = 512
ORDER = (2, 1, 3)
F32 = jnp.float32
BF16 = jnp.bfloat16


def nt(a, b):
    return lax.dot_general(a, b, (((1,), (1,)), ((), ())), preferred_element_type=F32)


def tn(a, b):
    return lax.dot_general(a, b, (((0,), (0,)), ((), ())), preferred_element_type=F32)


def exact(a, b, dims):
    return lax.dot_general(
        a, b, (dims, ((), ())), preferred_element_type=F32, precision=lax.Precision.HIGHEST
    )


def kernel(
    x_hbm, c_hbm, w_hbm, gain, keep,
    s_out, w_out,
    cot, cg, wg, xg, scaled, normed, acc, stat, wp, rsb, rsr, fb, sb, ci,
    loc, zs, zr, cs, cr, xs, xr, ps, pr, ws, wr, ts, tr, hs, hr, as_, ar, rs, rr, bs, br,
):
    sec = lax.axis_index("section")
    dp = lax.axis_index("dp")
    t = lax.axis_index("tensor")
    x, y = dp // 4, dp % 4

    def at(nx, ny, ntensor):
        return (sec, nx * 4 + ny, ntensor)

    def xp(k):
        return at((x + k) % 4, y, t)

    def yp(k):
        return at(x, (y + k) % 4, t)

    zp = at(x, y, 1 - t)
    to = at(2 * (x % 2) + y // 2, 2 * (1 - t) + y % 2, x // 2)
    back = at(2 * t + x // 2, 2 * (x % 2) + y % 2, 1 - y // 2)
    stat_peers = [(k, e) for e in (0, 1) for k in (2, 1, 3, 0) if (k, e) != (0, 0)]

    def remote(src, dst, ssem, rsem, dev):
        return pltpu.make_async_remote_copy(
            src_ref=src, dst_ref=dst, send_sem=ssem, recv_sem=rsem, device_id=dev,
            device_id_type=MESH,
        )

    sub = pl.multiple_of(t * 4096 + x * SUB, SUB)
    own_c = pltpu.make_async_copy(c_hbm.at[0], cot, loc.at[0])
    own_c.start()
    own_x = []
    for m in range(MB):
        cp = pltpu.make_async_copy(
            x_hbm.at[0, m, :, pl.ds(sub, SUB)], xg.at[m, x], loc.at[1 + m]
        )
        cp.start()
        own_x.append(cp)

    barrier = pltpu.get_barrier_semaphore()
    peers = [at((x + k) % 4, y, (t + e) % 2) for k, e in stat_peers]
    peers += [yp(k) for k in ORDER] + [to, back]
    peers += [((sec + 1) % 4, dp, t), ((sec + 3) % 4, dp, t)]
    for dev in peers:
        pl.semaphore_signal(barrier, inc=1, device_id=dev, device_id_type=MESH)
    own_c.wait()
    for m in range(MB):
        kept = keep[0, m, 0].astype(F32)
        cg[m, t, x] = (cot[m].astype(F32) * kept).astype(BF16)
    pl.semaphore_wait(barrier, len(peers))

    sends = []

    def go(cp):
        cp.start()
        sends.append(cp)
        return cp

    wto = remote(w_hbm.at[0], wg.at[2 * (1 - t) + y % 2], ps.at[0], pr.at[0], to)
    go(wto)
    zc = [
        go(remote(cg.at[m, t, x], cg.at[m, t, x], zs.at[m], zr.at[m], zp)) for m in range(MB)
    ]
    cgat = {}
    xat = {}

    def gather_cot(m, half, col):
        for i, k in enumerate(ORDER):
            cgat[m, half, i] = go(
                remote(cg.at[m, col, x], cg.at[m, col, x], cs.at[m, half, i], cr.at[m, half, i], xp(k))
            )

    def send_x(m):
        for i, k in enumerate(ORDER):
            start = pl.multiple_of(t * 4096 + ((x + k) % 4) * SUB, SUB)
            xat[m, i] = go(
                remote(
                    x_hbm.at[0, m, :, pl.ds(start, SUB)], xg.at[m, x], xs.at[m, i], xr.at[m, i], xp(k)
                )
            )

    gather_cot(0, 0, t)
    gather_cot(1, 0, t)
    send_x(0)
    for m in range(MB):
        zc[m].wait_recv()
        gather_cot(m, 1, 1 - t)
    send_x(1)
    wto.wait_recv()
    wgat = [
        go(remote(wg.at[y], wg.at[y], ws.at[i], wr.at[i], yp(k))) for i, k in enumerate(ORDER)
    ]

    lane_row = lax.broadcasted_iota(jnp.int32, (8, 128), 0)
    top_rows = jnp.where(lane_row < 4, 1.0, 0.0).astype(F32)
    low_rows = 1.0 - top_rows
    first_row = jnp.where(lane_row == 0, 1.0, 0.0).astype(F32)
    me = 2 * x + t

    def multiply(m):
        for half in range(2):
            for i in range(3):
                cgat[m, half, i].wait_recv()
        if m == 0:
            for cp in wgat:
                cp.wait_recv()
        own_x[m].wait()
        for i in range(3):
            xat[m, i].wait_recv()
        acc[...] = jnp.zeros_like(acc)

        def tile(i, carry):
            j = i // 2
            rows = pl.ds(pl.multiple_of((i % 2) * 256, 256), 256)
            cols = pl.ds(pl.multiple_of(i * 256, 256), 256)
            ng = nt(cg[m, 0].reshape(HALF, HALF), wg[2 + j, rows, :])
            ng += nt(cg[m, 1].reshape(HALF, HALF), wg[j, rows, :])
            g = gain[0:1, pl.ds(pl.multiple_of(sub + i * 256, 256), 256)]
            sc = ng * g
            scaled[m, :, cols] = sc
            xf = xg[m, :, :, cols].reshape(HALF, 256).astype(F32)
            pr_ = xf * sc
            sq = xf * xf
            acc[0] += pr_[:, :128] + pr_[:, 128:]
            acc[1] += sq[:, :128] + sq[:, 128:]
            return carry

        lax.fori_loop(0, 4, tile, 0)
        stat[m, me] = exact(top_rows, acc[0], ((1,), (1,))) + exact(low_rows, acc[1], ((1,), (1,)))
        return [
            go(
                remote(
                    stat.at[m, me], stat.at[m, me], ts.at[m, i], tr.at[m, i],
                    at((x + k) % 4, y, (t + e) % 2),
                )
            )
            for i, (k, e) in enumerate(stat_peers)
        ]

    def branch(m, arrivals):
        for cp in arrivals:
            cp.wait_recv()
        total = jnp.sum(stat[m], axis=0)
        dot_row = total[0:1]
        inv_row = lax.rsqrt(total[4:5] * (1.0 / D) + EPSILON)
        coef_row = inv_row * inv_row * inv_row * dot_row * (1.0 / D)
        acc[0] = exact(jnp.broadcast_to(inv_row, (8, HALF)), first_row, ((0,), (0,)))
        acc[1] = exact(jnp.broadcast_to(coef_row, (8, HALF)), first_row, ((0,), (0,)))

        def tile(i, carry):
            cols = pl.ds(pl.multiple_of(i * 128, 128), 128)
            g = gain[0:1, pl.ds(pl.multiple_of(sub + i * 128, 128), 128)]
            xf = xg[m, :, :, cols].reshape(HALF, 128).astype(F32)
            scaled[m, :, cols] = acc[0] * scaled[m, :, cols] - xf * acc[1]
            normed[m, :, cols] = (xf * acc[0] * g).astype(BF16)
            return carry

        lax.fori_loop(0, 8, tile, 0)

    below = (sec - 1, dp, t)
    chained = []
    final = {}

    def chain(m):
        for i, k in enumerate((2, 1, 3, 0)):
            xb = (x + k) % 4
            b = m * 4 + i
            cp = remote(sb.at[m, xb], ci.at[b], hs.at[b], hr.at[b], below)
            block = scaled.at[m, pl.ds(pl.multiple_of(xb * ROWS, ROWS), ROWS)]

            @pl.when(sec < 3)
            def _():
                cp.wait_recv()
                sb[m, xb] = (block[...] + ci[b].astype(F32)).astype(BF16)

            @pl.when(sec == 3)
            def _():
                sb[m, xb] = block[...].astype(BF16)

            @pl.when(sec > 0)
            def _():
                cp.start()

            chained.append(cp)
            spot = s_out.at[m, :, pl.ds(pl.multiple_of(x * SUB, SUB), SUB)]
            if k:
                final[m, i] = go(remote(sb.at[m, xb], spot, as_.at[m, i], ar.at[m, i], xp(k)))
            else:
                own = pltpu.make_async_copy(sb.at[m, xb], spot, loc.at[1 + m])
                own.start()
                final[m, i] = own

    def weights():
        def tile(i, carry):
            j = i // 2
            rows = pl.ds(pl.multiple_of((i % 2) * 256, 256), 256)
            cols = pl.ds(pl.multiple_of(i * 256, 256), 256)
            for c in range(2):
                part = tn(normed[0, :, cols], cg[0, c].reshape(HALF, HALF))
                part += tn(normed[1, :, cols], cg[1, c].reshape(HALF, HALF))
                wp[2 * (1 - c) + j, rows, :] = part
                rsb[2 * (1 - c) + j, rows, :] = part.astype(BF16)
            return carry

        lax.fori_loop(0, 4, tile, 0)
        return [
            go(remote(rsb.at[(y + k) % 4], rsr.at[i], rs.at[i], rr.at[i], yp(k)))
            for i, k in enumerate(ORDER)
        ]

    branch(0, multiply(0))
    chain(0)
    branch(1, multiply(1))
    reduced = weights()
    chain(1)
    for cp in reduced:
        cp.wait_recv()
    fb[...] = (
        wp[y] + rsr[0].astype(F32) + rsr[1].astype(F32) + rsr[2].astype(F32)
    ).astype(BF16)
    wback = go(remote(fb, w_out, bs.at[0], br.at[0], back))
    for m in range(MB):
        for i in range(3):
            final[m, i].wait_recv()
        final[m, 3].wait()
    wback.wait_recv()
    for cp in sends:
        cp.wait_send()
    for cp in chained:

        @pl.when(sec > 0)
        def _():
            cp.wait_send()


def on_device(layer_inputs, value_cotangent, value_weight, norm_gain, skip_keep, top_grad):
    any_ = pl.BlockSpec(memory_space=pl.ANY)
    dma = pltpu.SemaphoreType.DMA
    sums, weight = pl.pallas_call(
        kernel,
        name="backward",
        out_shape=(
            jax.ShapeDtypeStruct((MB, ROWS, 4096), BF16),
            jax.ShapeDtypeStruct((HALF, HALF), BF16),
        ),
        in_specs=[
            any_, any_, any_,
            pl.BlockSpec(memory_space=pltpu.VMEM),
            pl.BlockSpec(memory_space=pltpu.SMEM),
        ],
        out_specs=(any_, any_),
        scratch_shapes=[
            pltpu.VMEM((MB, ROWS, HALF), BF16),
            pltpu.VMEM((MB, 2, 4, ROWS, HALF), BF16),
            pltpu.VMEM((4, HALF, HALF), BF16),
            pltpu.VMEM((MB, 4, ROWS, SUB), BF16),
            pltpu.VMEM((MB, HALF, SUB), F32),
            pltpu.VMEM((MB, HALF, SUB), BF16),
            pltpu.VMEM((2, HALF, 128), F32),
            pltpu.VMEM((MB, 8, 8, HALF), F32),
            pltpu.VMEM((4, HALF, HALF), F32),
            pltpu.VMEM((4, HALF, HALF), BF16),
            pltpu.VMEM((3, HALF, HALF), BF16),
            pltpu.VMEM((HALF, HALF), BF16),
            pltpu.VMEM((MB, 4, ROWS, SUB), BF16),
            pltpu.VMEM((8, ROWS, SUB), BF16),
            dma((3,)),
            dma((MB,)), dma((MB,)),
            dma((MB, 2, 3)), dma((MB, 2, 3)),
            dma((MB, 3)), dma((MB, 3)),
            dma((1,)), dma((1,)),
            dma((3,)), dma((3,)),
            dma((MB, 7)), dma((MB, 7)),
            dma((8,)), dma((8,)),
            dma((MB, 3)), dma((MB, 3)),
            dma((3,)), dma((3,)),
            dma((1,)), dma((1,)),
        ],
        compiler_params=pltpu.CompilerParams(
            collective_id=0, has_side_effects=True, vmem_limit_bytes=56 * 1024 * 1024
        ),
    )(layer_inputs, value_cotangent, value_weight, norm_gain, skip_keep)
    total_rows = MB * ROWS * lax.axis_size("dp")
    factor = float(total_rows) ** (-0.5)
    grads = top_grad.astype(F32) + sums.astype(F32)
    return grads[None], (weight.astype(F32) * factor)[None]


def solution(mesh):
    placed = (
        P("section", None, "dp", None),
        P("section", None, "dp", "tensor"),
        P("section", "dp", "tensor"),
        P("section", None),
        P("section", None, "dp"),
        P(None, "dp", "tensor"),
    )
    return jax.shard_map(
        on_device,
        mesh=mesh,
        in_specs=placed,
        out_specs=(P("section", None, "dp", "tensor"), P("section", "dp", "tensor")),
        check_vma=False,
    )
```

time: 457 us -> 164 us (0.36)
  the two profiles are of different devices: /device:TPU:1 before, /device:TPU:8 now
where the time goes in v1:
time: 164 us
  Pallas kernels  156 us (95%)
  other arithmetic  5.47 us (3%)
    pallas_call x1, Pallas kernels, on_device(): pl.pallas_call(kernel, name='backward', out_shape=(jax.ShapeDtypeStruct((...  156 us
    broadcast_in_dim x2, other arithmetic, on_device(): return (grads[None], (weight.astype(F32) * factor)[None])  5.47 us

profile of v1, /device:TPU:8, one launch (start us, length us, event | category | flops | bytes accessed | tf_op | source)
XLA Modules:
  0.0 163.7 jit_solution(14102664129601287866)
XLA Ops:
  0.6 0.0 copy-start
  0.6 1.4 copy.8.keep
  2.1 156.1 %backward.1 = (bf16[2,128,4096]{2,1,0:T(8,128)(2,1)}, bf16[512,512]{1,0:T(8,128)(2,1)}) custom-call(bf16[1,2,128,8192]{3,2,1,0:T(8,128)(2,1)} %x_hbm.1, bf16[1,2,128,512]{3,2,1,0:T(8,128)(2,1)} %c_hbm.1, bf16[1,512,512]{2,1,0:T(8,128)(2,1)} %w_hbm.1, f32[1,8192]{1,0:T(1,128)} %gain.1, s32[1,2,1]{2,1,0:T(2,128)} %copy.8.keep), custom_call_target="tpu_custom_call" | custom-call | tf_op jit(solution)/shard_map/backward/pallas_call | solution.py:277
  158.2 0.0 copy-done
  158.2 0.0 copy-start.1
  158.2 4.4 %add_bitcast_fusion = f32[1,2,128,4096]{3,2,1,0:T(8,128)} fusion(bf16[2,128,4096]{2,1,0:T(8,128)(2,1)} %get-tuple-element.4, bf16[2,128,4096]{2,1,0:T(8,128)(2,1)S(1)} %copy-done), kind=kLoop, calls=%fused_computation | loop fusion | flops 3145728 | bytes 8388608 | tf_op jit(solution)/shard_map/broadcast_in_dim | solution.py:324
  162.6 0.0 copy-done.1
  162.6 1.1 multiply_bitcast_fusion
Async XLA Ops:
  0.6 157.6 %copy-start = (bf16[2,128,4096]{2,1,0:T(8,128)(2,1)S(1)}, bf16[2,128,4096]{2,1,0:T(8,128)(2,1)}, u32[]{:S(2)}) copy-start(bf16[2,128,4096]{2,1,0:T(8,128)(2,1)} %param.11) | copy-start | bytes 6291460
  158.2 4.4 %copy-start.1 = (bf16[512,512]{1,0:T(8,128)(2,1)S(1)}, bf16[512,512]{1,0:T(8,128)(2,1)}, u32[]{:S(2)}) copy-start(bf16[512,512]{1,0:T(8,128)(2,1)} %get-tuple-element.5) | copy-start | bytes 1572868

commit v2 on v1

--- a/solution.py
+++ b/solution.py
@@ -36,8 +36,8 @@
 def kernel(
     x_hbm, c_hbm, w_hbm, gain, keep,
     s_out, w_out,
-    cot, cg, wg, xg, scaled, normed, acc, stat, wp, rsb, rsr, fb, sb, ci,
-    loc, zs, zr, cs, cr, xs, xr, ps, pr, ws, wr, ts, tr, hs, hr, as_, ar, rs, rr, bs, br,
+    cot, cg, wg, xg, scaled, normed, acc, stat, wp, rsb, opp, rsr, fb, sb, ci,
+    loc, zs, zr, cs, cr, xs, xr, ps, pr, ws, wr, ts, tr, hs, hr, as_, ar, os_, or_, rs, rr, bs, br,
 ):
     sec = lax.axis_index("section")
     dp = lax.axis_index("dp")
@@ -53,10 +53,33 @@
     def yp(k):
         return at(x, (y + k) % 4, t)
 
+    def quarter(nx):
+        high = (nx // 2 + t) % 2
+        return (nx + high) % 2, high
+
     zp = at(x, y, 1 - t)
-    to = at(2 * (x % 2) + y // 2, 2 * (1 - t) + y % 2, x // 2)
-    back = at(2 * t + x // 2, 2 * (x % 2) + y % 2, 1 - y // 2)
+    to_t, row_high = x // 2, y // 2
+    crosses = (to_t + t) % 2
+    to_x = (x + 4 + row_high * (2 * (x % 2) - 1)) % 4
+    to_y = y + crosses * (3 - 2 * y)
+    to = at(to_x, to_y, to_t)
+    chip, high = quarter(x)
+    foreign = (y // 2 + high) % 2
+    back = at(2 * t + chip, y + foreign * (3 - 2 * y), t + foreign * (1 - 2 * t))
+    stays = (crosses + row_high) == 0
+    quart = 2 * chip + high
+    sub = pl.multiple_of(t * 4096 + quart * SUB, SUB)
     stat_peers = [(k, e) for e in (0, 1) for k in (2, 1, 3, 0) if (k, e) != (0, 0)]
+
+    def shard(slot):
+        far = (slot // 2 + high) % 2
+        col = t + far * (1 - 2 * t)
+        j = (slot + far) % 2
+        return col, j
+
+    def slot_of(far, j):
+        near = 2 * high + j
+        return near + far * (3 - 2 * near)
 
     def remote(src, dst, ssem, rsem, dev):
         return pltpu.make_async_remote_copy(
@@ -64,7 +87,6 @@
             device_id_type=MESH,
         )
 
-    sub = pl.multiple_of(t * 4096 + x * SUB, SUB)
     own_c = pltpu.make_async_copy(c_hbm.at[0], cot, loc.at[0])
     own_c.start()
     own_x = []
@@ -77,15 +99,21 @@
 
     barrier = pltpu.get_barrier_semaphore()
     peers = [at((x + k) % 4, y, (t + e) % 2) for k, e in stat_peers]
-    peers += [yp(k) for k in ORDER] + [to, back]
+    peers += [yp(k) for k in ORDER]
     peers += [((sec + 1) % 4, dp, t), ((sec + 3) % 4, dp, t)]
     for dev in peers:
         pl.semaphore_signal(barrier, inc=1, device_id=dev, device_id_type=MESH)
+
+    @pl.when(jnp.logical_not(stays))
+    def _():
+        for dev in (to, back):
+            pl.semaphore_signal(barrier, inc=1, device_id=dev, device_id_type=MESH)
+
     own_c.wait()
     for m in range(MB):
-        kept = keep[0, m, 0].astype(F32)
+        kept = keep[0, m].astype(F32)
         cg[m, t, x] = (cot[m].astype(F32) * kept).astype(BF16)
-    pl.semaphore_wait(barrier, len(peers))
+    pl.semaphore_wait(barrier, len(peers) + 2 - 2 * stays.astype(jnp.int32))
 
     sends = []
 
@@ -94,40 +122,100 @@
         sends.append(cp)
         return cp
 
-    wto = remote(w_hbm.at[0], wg.at[2 * (1 - t) + y % 2], ps.at[0], pr.at[0], to)
-    go(wto)
+    def moved(src, dst, lsem, ssem, rsem, dev):
+        local = pltpu.make_async_copy(src, dst, lsem)
+        far = remote(src, dst, ssem, rsem, dev)
+
+        @pl.when(stays)
+        def _():
+            local.start()
+
+        @pl.when(jnp.logical_not(stays))
+        def _():
+            far.start()
+
+        def arrive():
+            @pl.when(stays)
+            def _():
+                local.wait()
+
+            @pl.when(jnp.logical_not(stays))
+            def _():
+                far.wait_recv()
+
+        def leave():
+            @pl.when(jnp.logical_not(stays))
+            def _():
+                far.wait_send()
+
+        return arrive, leave
+
+    part = [pl.ds(0, 256), pl.ds(256, 256)]
+    left = (x + 3) % 4
+    right = (x + 1) % 4
+    wmove = [
+        moved(w_hbm.at[0, part[h]], wg.at[to_y, part[h]], loc.at[3 + h], ps.at[h], pr.at[h], to)
+        for h in range(2)
+    ]
     zc = [
         go(remote(cg.at[m, t, x], cg.at[m, t, x], zs.at[m], zr.at[m], zp)) for m in range(MB)
     ]
-    cgat = {}
+
+    def send_cot(m, half, i, col, origin, k):
+        return go(
+            remote(
+                cg.at[m, col, origin], cg.at[m, col, origin],
+                cs.at[m, half, i], cr.at[m, half, i], xp(k),
+            )
+        )
+
     xat = {}
-
-    def gather_cot(m, half, col):
-        for i, k in enumerate(ORDER):
-            cgat[m, half, i] = go(
-                remote(cg.at[m, col, x], cg.at[m, col, x], cs.at[m, half, i], cr.at[m, half, i], xp(k))
-            )
 
     def send_x(m):
         for i, k in enumerate(ORDER):
-            start = pl.multiple_of(t * 4096 + ((x + k) % 4) * SUB, SUB)
+            to_chip, to_high = quarter((x + k) % 4)
+            start = pl.multiple_of(t * 4096 + (2 * to_chip + to_high) * SUB, SUB)
             xat[m, i] = go(
                 remote(
                     x_hbm.at[0, m, :, pl.ds(start, SUB)], xg.at[m, x], xs.at[m, i], xr.at[m, i], xp(k)
                 )
             )
 
-    gather_cot(0, 0, t)
-    gather_cot(1, 0, t)
+    cat = {}
+    for m in range(MB):
+        cat[m, 0, 0] = send_cot(m, 0, 0, t, x, 1)
+        cat[m, 0, 1] = send_cot(m, 0, 1, t, x, 3)
+    got = set()
+
+    def wait_cot(key):
+        if key not in got:
+            got.add(key)
+            cat[key].wait_recv()
+
+    for m in range(MB):
+        zc[m].wait_recv()
+        cat[m, 1, 0] = send_cot(m, 1, 0, 1 - t, x, 1)
+        cat[m, 1, 1] = send_cot(m, 1, 1, 1 - t, x, 3)
     send_x(0)
     for m in range(MB):
-        zc[m].wait_recv()
-        gather_cot(m, 1, 1 - t)
+        wait_cot((m, 0, 0))
+        cat[m, 0, 2] = send_cot(m, 0, 2, t, left, 1)
+    wat = {}
+    for h in range(2):
+        wmove[h][0]()
+        for i, k in enumerate((1, 3)):
+            wat[h, i] = go(
+                remote(wg.at[y, part[h]], wg.at[y, part[h]], ws.at[h, i], wr.at[h, i], yp(k))
+            )
+    for m in range(MB):
+        wait_cot((m, 1, 1))
+        cat[m, 1, 2] = send_cot(m, 1, 2, 1 - t, right, 3)
     send_x(1)
-    wto.wait_recv()
-    wgat = [
-        go(remote(wg.at[y], wg.at[y], ws.at[i], wr.at[i], yp(k))) for i, k in enumerate(ORDER)
-    ]
+    for h, origin, k in ((0, (y + 3) % 4, 1), (1, (y + 1) % 4, 3)):
+        wat[h, h].wait_recv()
+        wat[h, 2] = go(
+            remote(wg.at[origin, part[h]], wg.at[origin, part[h]], ws.at[h, 2], wr.at[h, 2], yp(k))
+        )
 
     lane_row = lax.broadcasted_iota(jnp.int32, (8, 128), 0)
     top_rows = jnp.where(lane_row < 4, 1.0, 0.0).astype(F32)
@@ -138,10 +226,10 @@
     def multiply(m):
         for half in range(2):
             for i in range(3):
-                cgat[m, half, i].wait_recv()
+                wait_cot((m, half, i))
         if m == 0:
-            for cp in wgat:
-                cp.wait_recv()
+            for key in ((0, 1), (0, 2), (1, 0), (1, 2)):
+                wat[key].wait_recv()
         own_x[m].wait()
         for i in range(3):
             xat[m, i].wait_recv()
@@ -151,15 +239,15 @@
             j = i // 2
             rows = pl.ds(pl.multiple_of((i % 2) * 256, 256), 256)
             cols = pl.ds(pl.multiple_of(i * 256, 256), 256)
-            ng = nt(cg[m, 0].reshape(HALF, HALF), wg[2 + j, rows, :])
-            ng += nt(cg[m, 1].reshape(HALF, HALF), wg[j, rows, :])
+            ng = nt(cg[m, t].reshape(HALF, HALF), wg[slot_of(0, j), rows, :])
+            ng += nt(cg[m, 1 - t].reshape(HALF, HALF), wg[slot_of(1, j), rows, :])
             g = gain[0:1, pl.ds(pl.multiple_of(sub + i * 256, 256), 256)]
             sc = ng * g
             scaled[m, :, cols] = sc
             xf = xg[m, :, :, cols].reshape(HALF, 256).astype(F32)
-            pr_ = xf * sc
+            dot = xf * sc
             sq = xf * xf
-            acc[0] += pr_[:, :128] + pr_[:, 128:]
+            acc[0] += dot[:, :128] + dot[:, 128:]
             acc[1] += sq[:, :128] + sq[:, 128:]
             return carry
 
@@ -196,20 +284,30 @@
         lax.fori_loop(0, 8, tile, 0)
 
     below = (sec - 1, dp, t)
-    chained = []
+    chained = {}
     final = {}
-
-    def chain(m):
-        for i, k in enumerate((2, 1, 3, 0)):
+    spots = (2, 1, 3, 0)
+    for m in range(MB):
+        for i, k in enumerate(spots):
             xb = (x + k) % 4
             b = m * 4 + i
-            cp = remote(sb.at[m, xb], ci.at[b], hs.at[b], hr.at[b], below)
+            chained[m, i] = remote(sb.at[m, xb], ci.at[b], hs.at[b], hr.at[b], below)
+            spot = s_out.at[m, :, pl.ds(pl.multiple_of(quart * SUB, SUB), SUB)]
+            if k:
+                final[m, i] = remote(sb.at[m, xb], spot, as_.at[m, i], ar.at[m, i], xp(k))
+            else:
+                final[m, i] = pltpu.make_async_copy(sb.at[m, xb], spot, loc.at[1 + m])
+
+    def chain(m):
+        for i, k in enumerate(spots):
+            xb = (x + k) % 4
+            cp = chained[m, i]
             block = scaled.at[m, pl.ds(pl.multiple_of(xb * ROWS, ROWS), ROWS)]
 
             @pl.when(sec < 3)
             def _():
                 cp.wait_recv()
-                sb[m, xb] = (block[...] + ci[b].astype(F32)).astype(BF16)
+                sb[m, xb] = (block[...] + ci[m * 4 + i].astype(F32)).astype(BF16)
 
             @pl.when(sec == 3)
             def _():
@@ -219,52 +317,83 @@
             def _():
                 cp.start()
 
-            chained.append(cp)
-            spot = s_out.at[m, :, pl.ds(pl.multiple_of(x * SUB, SUB), SUB)]
-            if k:
-                final[m, i] = go(remote(sb.at[m, xb], spot, as_.at[m, i], ar.at[m, i], xp(k)))
+            final[m, i].start()
+
+    red = {}
+
+    def product(slot, h):
+        col, j = shard(slot)
+        cols = pl.ds(pl.multiple_of(j * HALF + h * 256, 256), 256)
+        total = tn(normed[0, :, cols], cg[0, col].reshape(HALF, HALF))
+        total += tn(normed[1, :, cols], cg[1, col].reshape(HALF, HALF))
+        return total
+
+    def pass_on(src, dst, i, k):
+        return go(remote(src, dst, rs.at[i], rr.at[i], yp(k)))
+
+    down, up, far_y = (y + 3) % 4, (y + 1) % 4, (y + 2) % 4
+
+    def weights():
+        for h, k in ((0, 1), (1, 3)):
+            rsb[2, h] = product(far_y, h).astype(BF16)
+            red["opp", h] = go(remote(rsb.at[2, h], opp.at[h], os_.at[h], or_.at[h], yp(k)))
+        for h in (1, 0):
+            wp[0, h] = product(up, h)
+            wp[1, h] = product(down, h)
+            if h == 1:
+                rsb[0, 1] = wp[0, 1].astype(BF16)
+                red[0, 1] = pass_on(rsb.at[0, 1], rsr.at[0, 1], 1, 1)
             else:
-                own = pltpu.make_async_copy(sb.at[m, xb], spot, loc.at[1 + m])
-                own.start()
-                final[m, i] = own
-
-    def weights():
-        def tile(i, carry):
-            j = i // 2
-            rows = pl.ds(pl.multiple_of((i % 2) * 256, 256), 256)
-            cols = pl.ds(pl.multiple_of(i * 256, 256), 256)
-            for c in range(2):
-                part = tn(normed[0, :, cols], cg[0, c].reshape(HALF, HALF))
-                part += tn(normed[1, :, cols], cg[1, c].reshape(HALF, HALF))
-                wp[2 * (1 - c) + j, rows, :] = part
-                rsb[2 * (1 - c) + j, rows, :] = part.astype(BF16)
-            return carry
-
-        lax.fori_loop(0, 4, tile, 0)
-        return [
-            go(remote(rsb.at[(y + k) % 4], rsr.at[i], rs.at[i], rr.at[i], yp(k)))
-            for i, k in enumerate(ORDER)
-        ]
+                rsb[1, 0] = wp[1, 0].astype(BF16)
+                red[1, 0] = pass_on(rsb.at[1, 0], rsr.at[1, 0], 2, 3)
+        for h in range(2):
+            wp[2, h] = product(y, h)
+        red["opp", 0].wait_recv()
+        rsb[0, 0] = (wp[0, 0] + opp[0].astype(F32)).astype(BF16)
+        red[0, 0] = pass_on(rsb.at[0, 0], rsr.at[0, 0], 0, 1)
+        red["opp", 1].wait_recv()
+        rsb[1, 1] = (wp[1, 1] + opp[1].astype(F32)).astype(BF16)
+        red[1, 1] = pass_on(rsb.at[1, 1], rsr.at[1, 1], 3, 3)
+
+    def finish():
+        moves = []
+        for h in range(2):
+            red[0, h].wait_recv()
+            red[1, h].wait_recv()
+            fb[h] = (wp[2, h] + rsr[0, h].astype(F32) + rsr[1, h].astype(F32)).astype(BF16)
+            moves.append(
+                moved(fb.at[h], w_out.at[part[h]], loc.at[3 + h], bs.at[h], br.at[h], back)
+            )
+        return moves
 
     branch(0, multiply(0))
-    chain(0)
+
+    @pl.when(sec >= 2)
+    def _():
+        chain(0)
+
     branch(1, multiply(1))
-    reduced = weights()
+    weights()
+
+    @pl.when(sec < 2)
+    def _():
+        chain(0)
+
     chain(1)
-    for cp in reduced:
-        cp.wait_recv()
-    fb[...] = (
-        wp[y] + rsr[0].astype(F32) + rsr[1].astype(F32) + rsr[2].astype(F32)
-    ).astype(BF16)
-    wback = go(remote(fb, w_out, bs.at[0], br.at[0], back))
+    returned = finish()
     for m in range(MB):
         for i in range(3):
             final[m, i].wait_recv()
+            final[m, i].wait_send()
         final[m, 3].wait()
-    wback.wait_recv()
+    for arrive, leave in returned:
+        arrive()
+        leave()
+    for _, leave in wmove:
+        leave()
     for cp in sends:
         cp.wait_send()
-    for cp in chained:
+    for cp in chained.values():
 
         @pl.when(sec > 0)
         def _():
@@ -296,28 +425,30 @@
             pltpu.VMEM((MB, HALF, SUB), BF16),
             pltpu.VMEM((2, HALF, 128), F32),
             pltpu.VMEM((MB, 8, 8, HALF), F32),
-            pltpu.VMEM((4, HALF, HALF), F32),
-            pltpu.VMEM((4, HALF, HALF), BF16),
-            pltpu.VMEM((3, HALF, HALF), BF16),
-            pltpu.VMEM((HALF, HALF), BF16),
+            pltpu.VMEM((3, 2, 256, HALF), F32),
+            pltpu.VMEM((3, 2, 256, HALF), BF16),
+            pltpu.VMEM((2, 256, HALF), BF16),
+            pltpu.VMEM((2, 2, 256, HALF), BF16),
+            pltpu.VMEM((2, 256, HALF), BF16),
             pltpu.VMEM((MB, 4, ROWS, SUB), BF16),
             pltpu.VMEM((8, ROWS, SUB), BF16),
-            dma((3,)),
+            dma((5,)),
             dma((MB,)), dma((MB,)),
             dma((MB, 2, 3)), dma((MB, 2, 3)),
             dma((MB, 3)), dma((MB, 3)),
-            dma((1,)), dma((1,)),
-            dma((3,)), dma((3,)),
+            dma((2,)), dma((2,)),
+            dma((2, 3)), dma((2, 3)),
             dma((MB, 7)), dma((MB, 7)),
             dma((8,)), dma((8,)),
             dma((MB, 3)), dma((MB, 3)),
-            dma((3,)), dma((3,)),
-            dma((1,)), dma((1,)),
+            dma((2,)), dma((2,)),
+            dma((4,)), dma((4,)),
+            dma((2,)), dma((2,)),
         ],
         compiler_params=pltpu.CompilerParams(
             collective_id=0, has_side_effects=True, vmem_limit_bytes=56 * 1024 * 1024
         ),
-    )(layer_inputs, value_cotangent, value_weight, norm_gain, skip_keep)
+    )(layer_inputs, value_cotangent, value_weight, norm_gain, skip_keep.reshape(1, MB))
     total_rows = MB * ROWS * lax.axis_size("dp")
     factor = float(total_rows) ** (-0.5)
     grads = top_grad.astype(F32) + sums.astype(F32)

time: 164 us -> 139 us (0.85)
  the two profiles are of different devices: /device:TPU:8 before, /device:TPU:4 now
where the time goes in v2:
time: 139 us; the launch traced here: 138 us
  Pallas kernels  132 us (95%)
  other arithmetic  5.5 us (4%)
    pallas_call x1, Pallas kernels, on_device(): pl.pallas_call(kernel, name='backward', out_shape=(jax.ShapeDtypeStruct((...  132 us
    broadcast_in_dim x2, other arithmetic, on_device(): return (grads[None], (weight.astype(F32) * factor)[None])  5.5 us

profile of v2, /device:TPU:4, one launch (start us, length us, event | category | flops | bytes accessed | tf_op | source)
XLA Modules:
  0.0 138.5 jit_solution(4324412180485769467)
XLA Ops:
  0.6 0.0 copy-start
  0.6 132.3 %backward.1 = (bf16[2,128,4096]{2,1,0:T(8,128)(2,1)}, bf16[512,512]{1,0:T(8,128)(2,1)}) custom-call(bf16[1,2,128,8192]{3,2,1,0:T(8,128)(2,1)} %x_hbm.1, bf16[1,2,128,512]{3,2,1,0:T(8,128)(2,1)} %c_hbm.1, bf16[1,512,512]{2,1,0:T(8,128)(2,1)} %w_hbm.1, f32[1,8192]{1,0:T(1,128)} %gain.1, s32[1,2]{1,0:T(1,128)} %bitcast.5), custom_call_target="tpu_custom_call" | custom-call | tf_op jit(solution)/shard_map/backward/pallas_call | solution.py:406
  132.9 0.0 copy-done
  133.0 0.0 copy-start.1
  133.0 4.4 %add_bitcast_fusion = f32[1,2,128,4096]{3,2,1,0:T(8,128)} fusion(bf16[2,128,4096]{2,1,0:T(8,128)(2,1)} %get-tuple-element.4, bf16[2,128,4096]{2,1,0:T(8,128)(2,1)S(1)} %copy-done), kind=kLoop, calls=%fused_computation | loop fusion | flops 3145728 | bytes 8388608 | tf_op jit(solution)/shard_map/broadcast_in_dim | solution.py:455
  137.4 0.0 copy-done.1
  137.4 1.1 multiply_bitcast_fusion
Async XLA Ops:
  0.6 132.3 %copy-start = (bf16[2,128,4096]{2,1,0:T(8,128)(2,1)S(1)}, bf16[2,128,4096]{2,1,0:T(8,128)(2,1)}, u32[]{:S(2)}) copy-start(bf16[2,128,4096]{2,1,0:T(8,128)(2,1)} %param.11) | copy-start | bytes 6291460
  133.0 4.4 %copy-start.1 = (bf16[512,512]{1,0:T(8,128)(2,1)S(1)}, bf16[512,512]{1,0:T(8,128)(2,1)}, u32[]{:S(2)}) copy-start(bf16[512,512]{1,0:T(8,128)(2,1)} %get-tuple-element.5) | copy-start | bytes 1572868

commit v3 on v1

v3 whole, which is shorter than its diff:
```python
import functools

import jax
import jax.numpy as jnp
from jax import lax
from jax.experimental import pallas as pl
from jax.experimental.pallas import tpu as pltpu
from jax.sharding import PartitionSpec as P

EPSILON = 1e-05
MESH = pl.DeviceIdType.MESH
MB = 2
ROWS = 128
D = 8192
SUB = 1024
HALF = 512
ORDER = (2, 1, 3)
F32 = jnp.float32
BF16 = jnp.bfloat16


def nt(a, b):
    return lax.dot_general(a, b, (((1,), (1,)), ((), ())), preferred_element_type=F32)


def tn(a, b):
    return lax.dot_general(a, b, (((0,), (0,)), ((), ())), preferred_element_type=F32)


def exact(a, b, dims):
    return lax.dot_general(
        a, b, (dims, ((), ())), preferred_element_type=F32, precision=lax.Precision.HIGHEST
    )


def kernel(
    x_hbm, c_hbm, w_hbm, gain, keep,
    s_out, w_out,
    cot, cg, wg, xg, scaled, normed, acc, stat, wp, rsi, opp, rso, rsr, fb, sb, ci,
    loc, zs, zr, cs, cr, xs, xr, ps, pr, ws, wr, ts, tr, hs, hr, as_, ar, os_, or_, rs, rr, bs, br,
):
    sec = lax.axis_index("section")
    dp = lax.axis_index("dp")
    t = lax.axis_index("tensor")
    x, y = dp // 4, dp % 4

    def at(nx, ny, ntensor):
        return (sec, nx * 4 + ny, ntensor)

    def yp(k):
        return at(x, (y + k) % 4, t)

    zp = at(x, y, 1 - t)
    odd = x % 2
    holds = (x // 2) == t
    lacks = jnp.logical_not(holds)
    here = holds.astype(jnp.int32) * (2 * odd - 1) + 1 - odd
    inner = at(x + 1 - 2 * odd, y, t)
    outer = at((x + 3 + 2 * odd) % 4, y, t)
    stat_peers = [(k, e) for e in (0, 1) for k in (2, 1, 3, 0) if (k, e) != (0, 0)]
    part = [pl.ds(0, 256), pl.ds(256, 256)]

    def feature(block, ny):
        return pl.multiple_of(t * 4096 + block * 2048 + ny * HALF, HALF)

    def remote(src, dst, ssem, rsem, dev):
        return pltpu.make_async_remote_copy(
            src_ref=src, dst_ref=dst, send_sem=ssem, recv_sem=rsem, device_id=dev,
            device_id_type=MESH,
        )

    own_c = pltpu.make_async_copy(c_hbm.at[0], cot, loc.at[0])
    own_c.start()
    own_w = pltpu.make_async_copy(w_hbm.at[0], wg.at[here, t], loc.at[1])

    @pl.when(holds)
    def _():
        own_w.start()

    own_x = {}
    for m in range(MB):
        for e in range(2):
            own_x[m, e] = pltpu.make_async_copy(
                x_hbm.at[0, m, :, pl.ds(feature(e, y), HALF)],
                xg.at[m, y, :, pl.ds(e * HALF, HALF)],
                loc.at[2 + 2 * m + e],
            )
            own_x[m, e].start()

    barrier = pltpu.get_barrier_semaphore()
    peers = [at(x, (y + k) % 4, (t + e) % 2) for k, e in stat_peers]
    peers += [inner, outer, ((sec + 1) % 4, dp, t), ((sec + 3) % 4, dp, t)]
    for dev in peers:
        pl.semaphore_signal(barrier, inc=1, device_id=dev, device_id_type=MESH)
    own_c.wait()
    for m in range(MB):
        kept = keep[0, m].astype(F32)
        cg[m, t, y] = (cot[m].astype(F32) * kept).astype(BF16)
    pl.semaphore_wait(barrier, len(peers))

    sends = []

    def go(cp):
        cp.start()
        sends.append(cp)
        return cp

    def send_cot(m, half, i, col, origin, k):
        return go(
            remote(
                cg.at[m, col, origin], cg.at[m, col, origin],
                cs.at[m, half, i], cr.at[m, half, i], yp(k),
            )
        )

    zc = []
    cat = {}
    for m in range(MB):
        zc.append(go(remote(cg.at[m, t, y], cg.at[m, t, y], zs.at[m], zr.at[m], zp)))
        cat[m, 0, 0] = send_cot(m, 0, 0, t, y, 1)
        cat[m, 0, 1] = send_cot(m, 0, 1, t, y, 3)
    got = set()

    def wait_cot(key):
        if key not in got:
            got.add(key)
            cat[key].wait_recv()

    wcross = [
        remote(w_hbm.at[0, part[h]], wg.at[odd, t, part[h]], ps.at[h], pr.at[h], zp)
        for h in range(2)
    ]

    @pl.when(lacks)
    def _():
        for h in range(2):
            wcross[h].start()

    win, wout = {}, {}
    for p in range(2):
        col = t if p == 0 else 1 - t
        for h in range(2):
            block = wg.at[here, col, part[h]]
            win[p, h] = remote(block, block, ws.at[p, h, 0], wr.at[p, h, 0], inner)
            wout[p, h] = remote(block, block, ws.at[p, h, 1], wr.at[p, h, 1], outer)

    def weight_step(p, h):
        @pl.when(holds)
        def _():
            if p == 1:
                wcross[h].wait_recv()
                wout[p, h].start()

        @pl.when(lacks)
        def _():
            wout[p, h].wait_recv()

        go(win[p, h])

    xat = {}

    def send_x(m):
        for i, k in enumerate(ORDER):
            for e in range(2):
                xat[m, i, e] = go(
                    remote(
                        x_hbm.at[0, m, :, pl.ds(feature(e, (y + k) % 4), HALF)],
                        xg.at[m, y, :, pl.ds(e * HALF, HALF)],
                        xs.at[m, i, e], xr.at[m, i, e], yp(k),
                    )
                )

    @pl.when(holds)
    def _():
        own_w.wait()
        wout[0, 0].start()
        wout[0, 1].start()

    up, down = (y + 1) % 4, (y + 3) % 4
    zc[0].wait_recv()
    cat[0, 1, 0] = send_cot(0, 1, 0, 1 - t, y, 1)
    cat[0, 1, 1] = send_cot(0, 1, 1, 1 - t, y, 3)
    wait_cot((0, 0, 0))
    cat[0, 0, 2] = send_cot(0, 0, 2, t, down, 1)
    weight_step(0, 0)
    zc[1].wait_recv()
    cat[1, 1, 0] = send_cot(1, 1, 0, 1 - t, y, 1)
    cat[1, 1, 1] = send_cot(1, 1, 1, 1 - t, y, 3)
    send_x(0)
    wait_cot((1, 0, 0))
    cat[1, 0, 2] = send_cot(1, 0, 2, t, down, 1)
    weight_step(0, 1)
    for m in range(MB):
        wait_cot((m, 1, 1))
        cat[m, 1, 2] = send_cot(m, 1, 2, 1 - t, up, 3)
    send_x(1)
    weight_step(1, 0)
    weight_step(1, 1)

    lane_row = lax.broadcasted_iota(jnp.int32, (8, 128), 0)
    top_rows = jnp.where(lane_row < 4, 1.0, 0.0).astype(F32)
    low_rows = 1.0 - top_rows
    first_row = jnp.where(lane_row == 0, 1.0, 0.0).astype(F32)
    me = 2 * y + t

    def multiply(m):
        for half in range(2):
            for i in range(3):
                wait_cot((m, half, i))
        if m == 0:
            for cp in win.values():
                cp.wait_recv()
        for e in range(2):
            own_x[m, e].wait()
            for i in range(3):
                xat[m, i, e].wait_recv()
        acc[...] = jnp.zeros_like(acc)

        def tile(i, carry):
            rows = pl.ds(pl.multiple_of((i % 2) * 256, 256), 256)
            cols = pl.ds(pl.multiple_of(i * 256, 256), 256)
            ng = nt(cg[m, 0].reshape(HALF, HALF), wg[i // 2, 0, rows, :])
            ng += nt(cg[m, 1].reshape(HALF, HALF), wg[i // 2, 1, rows, :])
            start = pl.multiple_of(feature(i // 2, y) + (i % 2) * 256, 256)
            sc = ng * gain[0:1, pl.ds(start, 256)]
            scaled[m, :, cols] = sc
            xf = xg[m, :, :, cols].reshape(HALF, 256).astype(F32)
            dot = xf * sc
            sq = xf * xf
            acc[0] += dot[:, :128] + dot[:, 128:]
            acc[1] += sq[:, :128] + sq[:, 128:]
            return carry

        lax.fori_loop(0, 4, tile, 0)
        stat[m, me] = exact(top_rows, acc[0], ((1,), (1,))) + exact(low_rows, acc[1], ((1,), (1,)))
        return [
            go(
                remote(
                    stat.at[m, me], stat.at[m, me], ts.at[m, i], tr.at[m, i],
                    at(x, (y + k) % 4, (t + e) % 2),
                )
            )
            for i, (k, e) in enumerate(stat_peers)
        ]

    def branch(m, arrivals):
        for cp in arrivals:
            cp.wait_recv()
        total = jnp.sum(stat[m], axis=0)
        dot_row = total[0:1]
        inv_row = lax.rsqrt(total[4:5] * (1.0 / D) + EPSILON)
        coef_row = inv_row * inv_row * inv_row * dot_row * (1.0 / D)
        acc[0] = exact(jnp.broadcast_to(inv_row, (8, HALF)), first_row, ((0,), (0,)))
        acc[1] = exact(jnp.broadcast_to(coef_row, (8, HALF)), first_row, ((0,), (0,)))

        def tile(i, carry):
            cols = pl.ds(pl.multiple_of(i * 128, 128), 128)
            start = pl.multiple_of(feature(i // 4, y) + (i % 4) * 128, 128)
            g = gain[0:1, pl.ds(start, 128)]
            xf = xg[m, :, :, cols].reshape(HALF, 128).astype(F32)
            scaled[m, :, cols] = acc[0] * scaled[m, :, cols] - xf * acc[1]
            normed[m, :, cols] = (xf * acc[0] * g).astype(BF16)
            return carry

        lax.fori_loop(0, 8, tile, 0)

    below = (sec - 1, dp, t)
    chained = {}
    final = {}
    spots = (2, 1, 3, 0)
    for m in range(MB):
        for i, k in enumerate(spots):
            yb = (y + k) % 4
            b = m * 4 + i
            chained[m, i] = remote(sb.at[m, yb], ci.at[b], hs.at[b], hr.at[b], below)
            for e in range(2):
                src = sb.at[m, yb, :, pl.ds(e * HALF, HALF)]
                spot = s_out.at[m, :, pl.ds(pl.multiple_of(e * 2048 + y * HALF, HALF), HALF)]
                if k:
                    final[m, i, e] = remote(src, spot, as_.at[m, i, e], ar.at[m, i, e], yp(k))
                else:
                    final[m, i, e] = pltpu.make_async_copy(src, spot, loc.at[2 + 2 * m + e])

    def chain(m, i):
        yb = (y + spots[i]) % 4
        cp = chained[m, i]
        block = scaled.at[m, pl.ds(pl.multiple_of(yb * ROWS, ROWS), ROWS)]

        @pl.when(sec < 3)
        def _():
            cp.wait_recv()
            sb[m, yb] = (block[...] + ci[m * 4 + i].astype(F32)).astype(BF16)

        @pl.when(sec == 3)
        def _():
            sb[m, yb] = block[...].astype(BF16)

        @pl.when(sec > 0)
        def _():
            cp.start()

    def deliver(m, i):
        for e in range(2):
            final[m, i, e].start()

    def product(block, p, h):
        col = 1 - t if p == 0 else t
        cols = pl.ds(pl.multiple_of(block * HALF + h * 256, 256), 256)
        total = tn(normed[0, :, cols], cg[0, col].reshape(HALF, HALF))
        total += tn(normed[1, :, cols], cg[1, col].reshape(HALF, HALF))
        return total

    steps = [(p, h) for p in range(2) for h in range(2)]
    rin, rout, ret, kept_here = {}, {}, {}, {}
    for p, h in steps:
        i = 2 * p + h
        rin[p, h] = remote(rsi.at[i], opp.at[i], rs.at[i], rr.at[i], inner)
        rout[p, h] = remote(rso.at[i], rsr.at[i], os_.at[i], or_.at[i], outer)
    for h in range(2):
        ret[h] = remote(fb.at[h], w_out.at[part[h]], bs.at[h], br.at[h], zp)
        kept_here[h] = pltpu.make_async_copy(fb.at[2 + h], w_out.at[part[h]], loc.at[6 + h])

    def weights():
        for p, h in steps:
            i = 2 * p + h
            rsi[i] = product(1 - here, p, h).astype(BF16)
            go(rin[p, h])
            wp[i] = product(here, p, h)

    def relay(p, h):
        i = 2 * p + h
        rin[p, h].wait_recv()

        @pl.when(lacks)
        def _():
            rso[i] = (wp[i] + opp[i].astype(F32)).astype(BF16)
            rout[p, h].start()

    def settle(p, h):
        i = 2 * p + h

        @pl.when(holds)
        def _():
            rout[p, h].wait_recv()
            fb[i] = (wp[i] + opp[i].astype(F32) + rsr[i].astype(F32)).astype(BF16)
            if p == 0:
                ret[h].start()
            else:
                kept_here[h].start()

    blocks = range(4)
    branch(0, multiply(0))

    @pl.when(sec >= 2)
    def _():
        for i in blocks:
            chain(0, i)

    arrivals = multiply(1)

    @pl.when(sec >= 2)
    def _():
        for i in blocks:
            deliver(0, i)

    branch(1, arrivals)
    weights()

    @pl.when(sec >= 2)
    def _():
        for i in blocks:
            chain(1, i)
            deliver(1, i)
        for n in range(4):
            relay(*steps[n])

    @pl.when(sec < 2)
    def _():
        for i in blocks:
            chain(0, i)
            deliver(0, i)
        for n in range(4):
            relay(*steps[n])
            chain(1, n)
            deliver(1, n)

    for step in steps:
        settle(*step)
    for (m, i, e), cp in final.items():
        if i < 3:
            cp.wait_recv()
            cp.wait_send()
        else:
            cp.wait()
    for cp in sends:
        cp.wait_send()

    @pl.when(holds)
    def _():
        for cp in list(wout.values()) + list(ret.values()):
            cp.wait_send()
        for h in range(2):
            kept_here[h].wait()

    @pl.when(lacks)
    def _():
        for cp in wcross + list(rout.values()):
            cp.wait_send()
        for h in range(2):
            ret[h].wait_recv()

    @pl.when(sec > 0)
    def _():
        for cp in chained.values():
            cp.wait_send()


def on_device(layer_inputs, value_cotangent, value_weight, norm_gain, skip_keep, top_grad):
    any_ = pl.BlockSpec(memory_space=pl.ANY)
    dma = pltpu.SemaphoreType.DMA
    sums, weight = pl.pallas_call(
        kernel,
        name="backward",
        out_shape=(
            jax.ShapeDtypeStruct((MB, ROWS, 4096), BF16),
            jax.ShapeDtypeStruct((HALF, HALF), BF16),
        ),
        in_specs=[
            any_, any_, any_,
            pl.BlockSpec(memory_space=pltpu.VMEM),
            pl.BlockSpec(memory_space=pltpu.SMEM),
        ],
        out_specs=(any_, any_),
        scratch_shapes=[
            pltpu.VMEM((MB, ROWS, HALF), BF16),
            pltpu.VMEM((MB, 2, 4, ROWS, HALF), BF16),
            pltpu.VMEM((2, 2, HALF, HALF), BF16),
            pltpu.VMEM((MB, 4, ROWS, SUB), BF16),
            pltpu.VMEM((MB, HALF, SUB), F32),
            pltpu.VMEM((MB, HALF, SUB), BF16),
            pltpu.VMEM((2, HALF, 128), F32),
            pltpu.VMEM((MB, 8, 8, HALF), F32),
            pltpu.VMEM((4, 256, HALF), F32),
            pltpu.VMEM((4, 256, HALF), BF16),
            pltpu.VMEM((4, 256, HALF), BF16),
            pltpu.VMEM((4, 256, HALF), BF16),
            pltpu.VMEM((4, 256, HALF), BF16),
            pltpu.VMEM((4, 256, HALF), BF16),
            pltpu.VMEM((MB, 4, ROWS, SUB), BF16),
            pltpu.VMEM((8, ROWS, SUB), BF16),
            dma((8,)),
            dma((MB,)), dma((MB,)),
            dma((MB, 2, 3)), dma((MB, 2, 3)),
            dma((MB, 3, 2)), dma((MB, 3, 2)),
            dma((2,)), dma((2,)),
            dma((2, 2, 2)), dma((2, 2, 2)),
            dma((MB, 7)), dma((MB, 7)),
            dma((8,)), dma((8,)),
            dma((MB, 3, 2)), dma((MB, 3, 2)),
            dma((4,)), dma((4,)),
            dma((4,)), dma((4,)),
            dma((2,)), dma((2,)),
        ],
        compiler_params=pltpu.CompilerParams(
            collective_id=0, has_side_effects=True, vmem_limit_bytes=56 * 1024 * 1024
        ),
    )(layer_inputs, value_cotangent, value_weight, norm_gain, skip_keep.reshape(1, MB))
    total_rows = MB * ROWS * lax.axis_size("dp")
    factor = float(total_rows) ** (-0.5)
    grads = top_grad.astype(F32) + sums.astype(F32)
    return grads[None], (weight.astype(F32) * factor)[None]


def solution(mesh):
    placed = (
        P("section", None, "dp", None),
        P("section", None, "dp", "tensor"),
        P("section", "dp", "tensor"),
        P("section", None),
        P("section", None, "dp"),
        P(None, "dp", "tensor"),
    )
    return jax.shard_map(
        on_device,
        mesh=mesh,
        in_specs=placed,
        out_specs=(P("section", None, "dp", "tensor"), P("section", "dp", "tensor")),
        check_vma=False,
    )
```

time: 164 us -> 116 us (0.71)
  the two profiles are of different devices: /device:TPU:8 before, /device:TPU:4 now
where the time goes in v3:
time: 116 us
  Pallas kernels  109 us (94%)
  other arithmetic  5.5 us (5%)
    pallas_call x1, Pallas kernels, on_device(): pl.pallas_call(kernel, name='backward', out_shape=(jax.ShapeDtypeStruct((...  109 us
    broadcast_in_dim x2, other arithmetic, on_device(): return (grads[None], (weight.astype(F32) * factor)[None])  5.5 us

profile of v3, /device:TPU:4, one launch (start us, length us, event | category | flops | bytes accessed | tf_op | source)
XLA Modules:
  0.0 115.6 jit_solution(4598445380908225728)
XLA Ops:
  0.6 0.0 copy-start
  0.6 109.4 %backward.1 = (bf16[2,128,4096]{2,1,0:T(8,128)(2,1)}, bf16[512,512]{1,0:T(8,128)(2,1)}) custom-call(bf16[1,2,128,8192]{3,2,1,0:T(8,128)(2,1)} %x_hbm.1, bf16[1,2,128,512]{3,2,1,0:T(8,128)(2,1)} %c_hbm.1, bf16[1,512,512]{2,1,0:T(8,128)(2,1)} %w_hbm.1, f32[1,8192]{1,0:T(1,128)} %gain.1, s32[1,2]{1,0:T(1,128)} %bitcast.5), custom_call_target="tpu_custom_call" | custom-call | tf_op jit(solution)/shard_map/backward/pallas_call | solution.py:421
  110.1 0.0 copy-done
  110.1 0.0 copy-start.1
  110.1 4.4 %add_bitcast_fusion = f32[1,2,128,4096]{3,2,1,0:T(8,128)} fusion(bf16[2,128,4096]{2,1,0:T(8,128)(2,1)} %get-tuple-element.4, bf16[2,128,4096]{2,1,0:T(8,128)(2,1)S(1)} %copy-done), kind=kLoop, calls=%fused_computation | loop fusion | flops 3145728 | bytes 8388608 | tf_op jit(solution)/shard_map/broadcast_in_dim | solution.py:471
  114.5 0.0 copy-done.1
  114.5 1.1 multiply_bitcast_fusion
Async XLA Ops:
  0.6 109.4 %copy-start = (bf16[2,128,4096]{2,1,0:T(8,128)(2,1)S(1)}, bf16[2,128,4096]{2,1,0:T(8,128)(2,1)}, u32[]{:S(2)}) copy-start(bf16[2,128,4096]{2,1,0:T(8,128)(2,1)} %param.11) | copy-start | bytes 6291460
  110.1 4.4 %copy-start.1 = (bf16[512,512]{1,0:T(8,128)(2,1)S(1)}, bf16[512,512]{1,0:T(8,128)(2,1)}, u32[]{:S(2)}) copy-start(bf16[512,512]{1,0:T(8,128)(2,1)} %get-tuple-element.5) | copy-start | bytes 1572868

commit v4 on v3

--- a/solution.py
+++ b/solution.py
@@ -36,8 +36,8 @@
 def kernel(
     x_hbm, c_hbm, w_hbm, gain, keep,
     s_out, w_out,
-    cot, cg, wg, xg, scaled, normed, acc, stat, wp, rsi, opp, rso, rsr, fb, sb, ci,
-    loc, zs, zr, cs, cr, xs, xr, ps, pr, ws, wr, ts, tr, hs, hr, as_, ar, os_, or_, rs, rr, bs, br,
+    cot, rowx, cg, wg, xg, scaled, normed, acc, invb, coefb, squares, stat, wp, rsi, opp, rso, rsr, fb, sb, ci,
+    loc, qs, qr, zs, zr, cs, cr, xs, xr, ps, pr, ws, wr, ts, tr, hs, hr, as_, ar, os_, or_, rs, rr, bs, br,
 ):
     sec = lax.axis_index("section")
     dp = lax.axis_index("dp")
@@ -86,6 +86,11 @@
                 loc.at[2 + 2 * m + e],
             )
             own_x[m, e].start()
+
+    own_rows = pltpu.make_async_copy(
+        x_hbm.at[0, :, :, pl.ds(pl.multiple_of(t * 4096, 4096), 4096)], rowx, loc.at[8]
+    )
+    own_rows.start()
 
     barrier = pltpu.get_barrier_semaphore()
     peers = [at(x, (y + k) % 4, (t + e) % 2) for k, e in stat_peers]
@@ -113,12 +118,30 @@
             )
         )
 
-    zc = []
     cat = {}
-    for m in range(MB):
-        zc.append(go(remote(cg.at[m, t, y], cg.at[m, t, y], zs.at[m], zr.at[m], zp)))
+    zc = [
+        go(remote(cg.at[m, t, y], cg.at[m, t, y], zs.at[m], zr.at[m], zp)) for m in range(MB)
+    ]
+
+    def send_own(m):
         cat[m, 0, 0] = send_cot(m, 0, 0, t, y, 1)
         cat[m, 0, 1] = send_cot(m, 0, 1, t, y, 3)
+
+    def send_other(m):
+        zc[m].wait_recv()
+        cat[m, 1, 0] = send_cot(m, 1, 0, 1 - t, y, 1)
+        cat[m, 1, 1] = send_cot(m, 1, 1, 1 - t, y, 3)
+
+    def pass_own(m):
+        wait_cot((m, 0, 0))
+        cat[m, 0, 2] = send_cot(m, 0, 2, t, down, 1)
+
+    def pass_other(m):
+        wait_cot((m, 1, 1))
+        cat[m, 1, 2] = send_cot(m, 1, 2, 1 - t, up, 3)
+
+    up, down = (y + 1) % 4, (y + 3) % 4
+    send_own(0)
     got = set()
 
     def wait_cot(key):
@@ -159,14 +182,15 @@
 
     xat = {}
 
-    def send_x(m):
+    def send_x(m, h):
         for i, k in enumerate(ORDER):
             for e in range(2):
-                xat[m, i, e] = go(
+                start = pl.multiple_of(feature(e, (y + k) % 4) + h * 256, 256)
+                xat[m, h, i, e] = go(
                     remote(
-                        x_hbm.at[0, m, :, pl.ds(feature(e, (y + k) % 4), HALF)],
-                        xg.at[m, y, :, pl.ds(e * HALF, HALF)],
-                        xs.at[m, i, e], xr.at[m, i, e], yp(k),
+                        x_hbm.at[0, m, :, pl.ds(start, 256)],
+                        xg.at[m, y, :, pl.ds(e * HALF + h * 256, 256)],
+                        xs.at[m, h, i, e], xr.at[m, h, i, e], yp(k),
                     )
                 )
 
@@ -176,32 +200,57 @@
         wout[0, 0].start()
         wout[0, 1].start()
 
-    up, down = (y + 1) % 4, (y + 3) % 4
-    zc[0].wait_recv()
-    cat[0, 1, 0] = send_cot(0, 1, 0, 1 - t, y, 1)
-    cat[0, 1, 1] = send_cot(0, 1, 1, 1 - t, y, 3)
-    wait_cot((0, 0, 0))
-    cat[0, 0, 2] = send_cot(0, 0, 2, t, down, 1)
-    weight_step(0, 0)
-    zc[1].wait_recv()
-    cat[1, 1, 0] = send_cot(1, 1, 0, 1 - t, y, 1)
-    cat[1, 1, 1] = send_cot(1, 1, 1, 1 - t, y, 3)
-    send_x(0)
-    wait_cot((1, 0, 0))
-    cat[1, 0, 2] = send_cot(1, 0, 2, t, down, 1)
-    weight_step(0, 1)
-    for m in range(MB):
-        wait_cot((m, 1, 1))
-        cat[m, 1, 2] = send_cot(m, 1, 2, 1 - t, up, 3)
-    send_x(1)
-    weight_step(1, 0)
-    weight_step(1, 1)
-
+    send_x(0, 0)
     lane_row = lax.broadcasted_iota(jnp.int32, (8, 128), 0)
-    top_rows = jnp.where(lane_row < 4, 1.0, 0.0).astype(F32)
-    low_rows = 1.0 - top_rows
+    ones = jnp.ones((8, 128), F32)
     first_row = jnp.where(lane_row == 0, 1.0, 0.0).astype(F32)
     me = 2 * y + t
+
+    def tell(src, slots, ssem, rsem):
+        return [
+            go(
+                remote(
+                    src, slots, ssem.at[i], rsem.at[i], at(x, (y + k) % 4, (t + e) % 2)
+                )
+            )
+            for i, (k, e) in enumerate(stat_peers)
+        ]
+
+    own_rows.wait()
+    for m in range(MB):
+
+        def square(i, total):
+            xf = rowx[m, :, pl.ds(pl.multiple_of(i * 512, 512), 512)].astype(F32)
+            xf = xf * xf
+            return total + (xf[:, :128] + xf[:, 128:256]) + (xf[:, 256:384] + xf[:, 384:])
+
+        total = lax.fori_loop(0, 8, square, jnp.zeros((ROWS, 128), F32))
+        squares[me, :, m * ROWS : (m + 1) * ROWS] = exact(ones, total, ((1,), (1,)))
+    sums = tell(squares.at[me], squares.at[me], qs, qr)
+
+    send_other(0)
+    pass_own(0)
+    send_x(0, 1)
+    weight_step(0, 0)
+    send_own(1)
+    send_other(1)
+    pass_other(0)
+    weight_step(0, 1)
+    pass_own(1)
+    send_x(1, 0)
+    pass_other(1)
+    weight_step(1, 0)
+    send_x(1, 1)
+    weight_step(1, 1)
+
+    for cp in sums:
+        cp.wait_recv()
+    for n in range(4):
+        total = squares[2 * n] + squares[2 * n + 1]
+        inv = lax.rsqrt(total * (1.0 / D) + EPSILON)
+        wide = exact(inv, first_row, ((0,), (0,)))
+        for m in range(MB):
+            invb[m, n] = wide[m * ROWS : (m + 1) * ROWS]
 
     def multiply(m):
         for half in range(2):
@@ -210,11 +259,6 @@
         if m == 0:
             for cp in win.values():
                 cp.wait_recv()
-        for e in range(2):
-            own_x[m, e].wait()
-            for i in range(3):
-                xat[m, i, e].wait_recv()
-        acc[...] = jnp.zeros_like(acc)
 
         def tile(i, carry):
             rows = pl.ds(pl.multiple_of((i % 2) * 256, 256), 256)
@@ -222,47 +266,45 @@
             ng = nt(cg[m, 0].reshape(HALF, HALF), wg[i // 2, 0, rows, :])
             ng += nt(cg[m, 1].reshape(HALF, HALF), wg[i // 2, 1, rows, :])
             start = pl.multiple_of(feature(i // 2, y) + (i % 2) * 256, 256)
-            sc = ng * gain[0:1, pl.ds(start, 256)]
-            scaled[m, :, cols] = sc
-            xf = xg[m, :, :, cols].reshape(HALF, 256).astype(F32)
-            dot = xf * sc
-            sq = xf * xf
-            acc[0] += dot[:, :128] + dot[:, 128:]
-            acc[1] += sq[:, :128] + sq[:, 128:]
+            scaled[m, :, cols] = ng * gain[0:1, pl.ds(start, 256)]
             return carry
 
         lax.fori_loop(0, 4, tile, 0)
-        stat[m, me] = exact(top_rows, acc[0], ((1,), (1,))) + exact(low_rows, acc[1], ((1,), (1,)))
-        return [
-            go(
-                remote(
-                    stat.at[m, me], stat.at[m, me], ts.at[m, i], tr.at[m, i],
-                    at(x, (y + k) % 4, (t + e) % 2),
-                )
-            )
-            for i, (k, e) in enumerate(stat_peers)
-        ]
-
-    def branch(m, arrivals):
+
+    def inputs(m, h):
+        if h == 0:
+            for e in range(2):
+                own_x[m, e].wait()
+        for e in range(2):
+            for i in range(3):
+                xat[m, h, i, e].wait_recv()
+        inv = invb[m].reshape(HALF, 128)
+
+        def tile(i, total):
+            at_col = pl.multiple_of((i // 2) * HALF + h * 256 + (i % 2) * 128, 128)
+            cols = pl.ds(at_col, 128)
+            start = pl.multiple_of(feature(i // 2, y) + h * 256 + (i % 2) * 128, 128)
+            xf = xg[m, :, :, cols].reshape(HALF, 128).astype(F32)
+            normed[m, :, cols] = (xf * inv * gain[0:1, pl.ds(start, 128)]).astype(BF16)
+            if h == 0:
+                acc[...] = jnp.where(i == 0, 0.0, acc[...]) + xf * scaled[m, :, cols]
+            else:
+                acc[...] += xf * scaled[m, :, cols]
+            return total
+
+        lax.fori_loop(0, 4, tile, 0)
+
+    def share(m):
+        stat[m, me] = exact(ones, acc[...], ((1,), (1,)))
+        return tell(stat.at[m, me], stat.at[m, me], ts.at[m], tr.at[m])
+
+    def coefficients(m, arrivals):
         for cp in arrivals:
             cp.wait_recv()
-        total = jnp.sum(stat[m], axis=0)
-        dot_row = total[0:1]
-        inv_row = lax.rsqrt(total[4:5] * (1.0 / D) + EPSILON)
-        coef_row = inv_row * inv_row * inv_row * dot_row * (1.0 / D)
-        acc[0] = exact(jnp.broadcast_to(inv_row, (8, HALF)), first_row, ((0,), (0,)))
-        acc[1] = exact(jnp.broadcast_to(coef_row, (8, HALF)), first_row, ((0,), (0,)))
-
-        def tile(i, carry):
-            cols = pl.ds(pl.multiple_of(i * 128, 128), 128)
-            start = pl.multiple_of(feature(i // 4, y) + (i % 4) * 128, 128)
-            g = gain[0:1, pl.ds(start, 128)]
-            xf = xg[m, :, :, cols].reshape(HALF, 128).astype(F32)
-            scaled[m, :, cols] = acc[0] * scaled[m, :, cols] - xf * acc[1]
-            normed[m, :, cols] = (xf * acc[0] * g).astype(BF16)
-            return carry
-
-        lax.fori_loop(0, 8, tile, 0)
+        total = jnp.sum(stat[m], axis=0) * (1.0 / D)
+        dots = exact(total, first_row, ((0,), (0,)))
+        inv = invb[m].reshape(HALF, 128)
+        coefb[m] = (inv * inv * inv * dots).reshape(4, ROWS, 128)
 
     below = (sec - 1, dp, t)
     chained = {}
@@ -284,16 +326,28 @@
     def chain(m, i):
         yb = (y + spots[i]) % 4
         cp = chained[m, i]
-        block = scaled.at[m, pl.ds(pl.multiple_of(yb * ROWS, ROWS), ROWS)]
+        rows = pl.ds(pl.multiple_of(yb * ROWS, ROWS), ROWS)
+
+        def put(above):
+            def tile(n, carry):
+                cols = pl.ds(pl.multiple_of(n * 128, 128), 128)
+                xf = xg[m, yb, :, cols].astype(F32)
+                value = invb[m, yb] * scaled[m, rows, cols] - xf * coefb[m, yb]
+                if above:
+                    value += ci[m * 4 + i, :, cols].astype(F32)
+                sb[m, yb, :, cols] = value.astype(BF16)
+                return carry
+
+            lax.fori_loop(0, 8, tile, 0)
 
         @pl.when(sec < 3)
         def _():
             cp.wait_recv()
-            sb[m, yb] = (block[...] + ci[m * 4 + i].astype(F32)).astype(BF16)
+            put(True)
 
         @pl.when(sec == 3)
         def _():
-            sb[m, yb] = block[...].astype(BF16)
+            put(False)
 
         @pl.when(sec > 0)
         def _():
@@ -310,7 +364,7 @@
         total += tn(normed[1, :, cols], cg[1, col].reshape(HALF, HALF))
         return total
 
-    steps = [(p, h) for p in range(2) for h in range(2)]
+    steps = [(p, h) for h in range(2) for p in range(2)]
     rin, rout, ret, kept_here = {}, {}, {}, {}
     for p, h in steps:
         i = 2 * p + h
@@ -320,8 +374,8 @@
         ret[h] = remote(fb.at[h], w_out.at[part[h]], bs.at[h], br.at[h], zp)
         kept_here[h] = pltpu.make_async_copy(fb.at[2 + h], w_out.at[part[h]], loc.at[6 + h])
 
-    def weights():
-        for p, h in steps:
+    def weights(h):
+        for p in range(2):
             i = 2 * p + h
             rsi[i] = product(1 - here, p, h).astype(BF16)
             go(rin[p, h])
@@ -349,29 +403,38 @@
                 kept_here[h].start()
 
     blocks = range(4)
-    branch(0, multiply(0))
+    multiply(0)
+    inputs(0, 0)
+    inputs(0, 1)
+    arrivals = share(0)
+    multiply(1)
+    coefficients(0, arrivals)
 
     @pl.when(sec >= 2)
     def _():
         for i in blocks:
             chain(0, i)
 
-    arrivals = multiply(1)
+    inputs(1, 0)
+    weights(0)
+    inputs(1, 1)
+    arrivals = share(1)
 
     @pl.when(sec >= 2)
     def _():
         for i in blocks:
             deliver(0, i)
 
-    branch(1, arrivals)
-    weights()
+    weights(1)
+    relay(*steps[0])
+    coefficients(1, arrivals)
 
     @pl.when(sec >= 2)
     def _():
         for i in blocks:
             chain(1, i)
             deliver(1, i)
-        for n in range(4):
+        for n in (1, 2, 3):
             relay(*steps[n])
 
     @pl.when(sec < 2)
@@ -379,10 +442,12 @@
         for i in blocks:
             chain(0, i)
             deliver(0, i)
-        for n in range(4):
+        for n in (1, 2, 3):
             relay(*steps[n])
-            chain(1, n)
-            deliver(1, n)
+            chain(1, n - 1)
+            deliver(1, n - 1)
+        chain(1, 3)
+        deliver(1, 3)
 
     for step in steps:
         settle(*step)
@@ -433,12 +498,16 @@
         out_specs=(any_, any_),
         scratch_shapes=[
             pltpu.VMEM((MB, ROWS, HALF), BF16),
+            pltpu.VMEM((MB, ROWS, 4096), BF16),
             pltpu.VMEM((MB, 2, 4, ROWS, HALF), BF16),
             pltpu.VMEM((2, 2, HALF, HALF), BF16),
             pltpu.VMEM((MB, 4, ROWS, SUB), BF16),
             pltpu.VMEM((MB, HALF, SUB), F32),
             pltpu.VMEM((MB, HALF, SUB), BF16),
-            pltpu.VMEM((2, HALF, 128), F32),
+            pltpu.VMEM((HALF, 128), F32),
+            pltpu.VMEM((MB, 4, ROWS, 128), F32),
+            pltpu.VMEM((MB, 4, ROWS, 128), F32),
+            pltpu.VMEM((8, 8, 2 * ROWS), F32),
             pltpu.VMEM((MB, 8, 8, HALF), F32),
             pltpu.VMEM((4, 256, HALF), F32),
             pltpu.VMEM((4, 256, HALF), BF16),
@@ -448,10 +517,11 @@
             pltpu.VMEM((4, 256, HALF), BF16),
             pltpu.VMEM((MB, 4, ROWS, SUB), BF16),
             pltpu.VMEM((8, ROWS, SUB), BF16),
-            dma((8,)),
+            dma((9,)),
+            dma((7,)), dma((7,)),
             dma((MB,)), dma((MB,)),
             dma((MB, 2, 3)), dma((MB, 2, 3)),
-            dma((MB, 3, 2)), dma((MB, 3, 2)),
+            dma((MB, 2, 3, 2)), dma((MB, 2, 3, 2)),
             dma((2,)), dma((2,)),
             dma((2, 2, 2)), dma((2, 2, 2)),
             dma((MB, 7)), dma((MB, 7)),

time: 116 us -> 119 us (1.026)
  Pallas kernels: 109 us -> 112 us
    pallas_call x1, Pallas kernels: 109 us -> 112 us  [on_device(): pl.pallas_call(kernel, name='backward', out_shape=(jax.ShapeDtypeStruct((...]
where the time goes in v4:
time: 119 us
  Pallas kernels  112 us (94%)
  other arithmetic  5.5 us (5%)
    pallas_call x1, Pallas kernels, on_device(): pl.pallas_call(kernel, name='backward', out_shape=(jax.ShapeDtypeStruct((...  112 us
    broadcast_in_dim x2, other arithmetic, on_device(): return (grads[None], (weight.astype(F32) * factor)[None])  5.5 us

profile of v4, /device:TPU:4, one launch (start us, length us, event | category | flops | bytes accessed | tf_op | source)
XLA Modules:
  0.0 118.5 jit_solution(9106723668786856778)
XLA Ops:
  0.6 0.0 copy-start
  0.6 112.3 %backward.1 = (bf16[2,128,4096]{2,1,0:T(8,128)(2,1)}, bf16[512,512]{1,0:T(8,128)(2,1)}) custom-call(bf16[1,2,128,8192]{3,2,1,0:T(8,128)(2,1)} %x_hbm.1, bf16[1,2,128,512]{3,2,1,0:T(8,128)(2,1)} %c_hbm.1, bf16[1,512,512]{2,1,0:T(8,128)(2,1)} %w_hbm.1, f32[1,8192]{1,0:T(1,128)} %gain.1, s32[1,2]{1,0:T(1,128)} %bitcast.5), custom_call_target="tpu_custom_call" | custom-call | tf_op jit(solution)/shard_map/backward/pallas_call | solution.py:486
  113.0 0.0 copy-done
  113.0 0.0 copy-start.1
  113.0 4.4 %add_bitcast_fusion = f32[1,2,128,4096]{3,2,1,0:T(8,128)} fusion(bf16[2,128,4096]{2,1,0:T(8,128)(2,1)} %get-tuple-element.4, bf16[2,128,4096]{2,1,0:T(8,128)(2,1)S(1)} %copy-done), kind=kLoop, calls=%fused_computation | loop fusion | flops 3145728 | bytes 8388608 | tf_op jit(solution)/shard_map/broadcast_in_dim | solution.py:541
  117.4 0.0 copy-done.1
  117.4 1.1 multiply_bitcast_fusion
Async XLA Ops:
  0.6 112.4 %copy-start = (bf16[2,128,4096]{2,1,0:T(8,128)(2,1)S(1)}, bf16[2,128,4096]{2,1,0:T(8,128)(2,1)}, u32[]{:S(2)}) copy-start(bf16[2,128,4096]{2,1,0:T(8,128)(2,1)} %param.11) | copy-start | bytes 6291460
  113.0 4.4 %copy-start.1 = (bf16[512,512]{1,0:T(8,128)(2,1)S(1)}, bf16[512,512]{1,0:T(8,128)(2,1)}, u32[]{:S(2)}) copy-start(bf16[512,512]{1,0:T(8,128)(2,1)} %get-tuple-element.5) | copy-start | bytes 1572868

commit v5 on v4

--- a/solution.py
+++ b/solution.py
@@ -119,9 +119,10 @@
         )
 
     cat = {}
-    zc = [
-        go(remote(cg.at[m, t, y], cg.at[m, t, y], zs.at[m], zr.at[m], zp)) for m in range(MB)
-    ]
+    zc = {}
+
+    def send_z(m):
+        zc[m] = go(remote(cg.at[m, t, y], cg.at[m, t, y], zs.at[m], zr.at[m], zp))
 
     def send_own(m):
         cat[m, 0, 0] = send_cot(m, 0, 0, t, y, 1)
@@ -141,7 +142,6 @@
         cat[m, 1, 2] = send_cot(m, 1, 2, 1 - t, up, 3)
 
     up, down = (y + 1) % 4, (y + 3) % 4
-    send_own(0)
     got = set()
 
     def wait_cot(key):
@@ -149,36 +149,30 @@
             got.add(key)
             cat[key].wait_recv()
 
-    wcross = [
-        remote(w_hbm.at[0, part[h]], wg.at[odd, t, part[h]], ps.at[h], pr.at[h], zp)
-        for h in range(2)
-    ]
-
-    @pl.when(lacks)
-    def _():
-        for h in range(2):
-            wcross[h].start()
-
-    win, wout = {}, {}
-    for p in range(2):
-        col = t if p == 0 else 1 - t
-        for h in range(2):
-            block = wg.at[here, col, part[h]]
-            win[p, h] = remote(block, block, ws.at[p, h, 0], wr.at[p, h, 0], inner)
-            wout[p, h] = remote(block, block, ws.at[p, h, 1], wr.at[p, h, 1], outer)
-
-    def weight_step(p, h):
-        @pl.when(holds)
-        def _():
-            if p == 1:
-                wcross[h].wait_recv()
-                wout[p, h].start()
+    pieces = [(p, 128 * n, 128) for p in range(2) for n in range(4)]
+    wcross, win, wout = {}, {}, {}
+    for n, (p, first, size) in enumerate(pieces):
+        rows = pl.ds(first, size)
+        if p:
+            wcross[n] = remote(
+                w_hbm.at[0, rows], wg.at[odd, t, rows], ps.at[n], pr.at[n], zp
+            )
+        block = wg.at[here, 1 - t if p else t, rows]
+        win[n] = remote(block, block, ws.at[n, 0], wr.at[n, 0], inner)
+        wout[n] = remote(block, block, ws.at[n, 1], wr.at[n, 1], outer)
+
+    def weight_step(n):
+        if n in wcross:
+            @pl.when(holds)
+            def _():
+                wcross[n].wait_recv()
+                wout[n].start()
+                win[n].start()
 
         @pl.when(lacks)
         def _():
-            wout[p, h].wait_recv()
-
-        go(win[p, h])
+            wout[n].wait_recv()
+            win[n].start()
 
     xat = {}
 
@@ -197,10 +191,19 @@
     @pl.when(holds)
     def _():
         own_w.wait()
-        wout[0, 0].start()
-        wout[0, 1].start()
-
-    send_x(0, 0)
+        for n in range(4):
+            wout[n].start()
+            win[n].start()
+
+    for m in range(MB):
+        send_z(m)
+        send_own(m)
+
+    @pl.when(lacks)
+    def _():
+        for cp in wcross.values():
+            cp.start()
+
     lane_row = lax.broadcasted_iota(jnp.int32, (8, 128), 0)
     ones = jnp.ones((8, 128), F32)
     first_row = jnp.where(lane_row == 0, 1.0, 0.0).astype(F32)
@@ -228,20 +231,24 @@
         squares[me, :, m * ROWS : (m + 1) * ROWS] = exact(ones, total, ((1,), (1,)))
     sums = tell(squares.at[me], squares.at[me], qs, qr)
 
+    weight_step(0)
     send_other(0)
     pass_own(0)
+    weight_step(1)
+    send_other(1)
+    pass_own(1)
+    send_x(0, 0)
+    weight_step(2)
+    weight_step(3)
+    pass_other(0)
     send_x(0, 1)
-    weight_step(0, 0)
-    send_own(1)
-    send_other(1)
-    pass_other(0)
-    weight_step(0, 1)
-    pass_own(1)
+    weight_step(4)
+    pass_other(1)
     send_x(1, 0)
-    pass_other(1)
-    weight_step(1, 0)
+    weight_step(5)
+    weight_step(6)
+    weight_step(7)
     send_x(1, 1)
-    weight_step(1, 1)
 
     for cp in sums:
         cp.wait_recv()
@@ -252,10 +259,12 @@
         for m in range(MB):
             invb[m, n] = wide[m * ROWS : (m + 1) * ROWS]
 
-    def multiply(m):
+    def cotangent(m):
         for half in range(2):
             for i in range(3):
                 wait_cot((m, half, i))
+
+    def multiply(m):
         if m == 0:
             for cp in win.values():
                 cp.wait_recv()
@@ -280,19 +289,26 @@
                 xat[m, h, i, e].wait_recv()
         inv = invb[m].reshape(HALF, 128)
 
-        def tile(i, total):
+        def tile(i, carry):
             at_col = pl.multiple_of((i // 2) * HALF + h * 256 + (i % 2) * 128, 128)
             cols = pl.ds(at_col, 128)
             start = pl.multiple_of(feature(i // 2, y) + h * 256 + (i % 2) * 128, 128)
             xf = xg[m, :, :, cols].reshape(HALF, 128).astype(F32)
             normed[m, :, cols] = (xf * inv * gain[0:1, pl.ds(start, 128)]).astype(BF16)
-            if h == 0:
-                acc[...] = jnp.where(i == 0, 0.0, acc[...]) + xf * scaled[m, :, cols]
-            else:
-                acc[...] += xf * scaled[m, :, cols]
-            return total
+            return carry
 
         lax.fori_loop(0, 4, tile, 0)
+
+    def dots(m):
+        acc[...] = jnp.zeros_like(acc)
+
+        def tile(i, carry):
+            cols = pl.ds(pl.multiple_of(i * 128, 128), 128)
+            xf = xg[m, :, :, cols].reshape(HALF, 128).astype(F32)
+            acc[...] += xf * scaled[m, :, cols]
+            return carry
+
+        lax.fori_loop(0, 8, tile, 0)
 
     def share(m):
         stat[m, me] = exact(ones, acc[...], ((1,), (1,)))
@@ -302,9 +318,9 @@
         for cp in arrivals:
             cp.wait_recv()
         total = jnp.sum(stat[m], axis=0) * (1.0 / D)
-        dots = exact(total, first_row, ((0,), (0,)))
+        wide = exact(total, first_row, ((0,), (0,)))
         inv = invb[m].reshape(HALF, 128)
-        coefb[m] = (inv * inv * inv * dots).reshape(4, ROWS, 128)
+        coefb[m] = (inv * inv * inv * wide).reshape(4, ROWS, 128)
 
     below = (sec - 1, dp, t)
     chained = {}
@@ -403,10 +419,18 @@
                 kept_here[h].start()
 
     blocks = range(4)
+
+    def block(m, i):
+        chain(m, i)
+        deliver(m, i)
+
+    cotangent(0)
     multiply(0)
     inputs(0, 0)
     inputs(0, 1)
+    dots(0)
     arrivals = share(0)
+    cotangent(1)
     multiply(1)
     coefficients(0, arrivals)
 
@@ -418,13 +442,8 @@
     inputs(1, 0)
     weights(0)
     inputs(1, 1)
+    dots(1)
     arrivals = share(1)
-
-    @pl.when(sec >= 2)
-    def _():
-        for i in blocks:
-            deliver(0, i)
-
     weights(1)
     relay(*steps[0])
     coefficients(1, arrivals)
@@ -433,31 +452,40 @@
     def _():
         for i in blocks:
             chain(1, i)
-            deliver(1, i)
-        for n in (1, 2, 3):
-            relay(*steps[n])
+        for m in range(MB):
+            for i in blocks:
+                deliver(m, i)
+        relay(*steps[1])
+        settle(*steps[0])
+        relay(*steps[2])
+        settle(*steps[1])
+        relay(*steps[3])
+        settle(*steps[2])
+        settle(*steps[3])
 
     @pl.when(sec < 2)
     def _():
         for i in blocks:
-            chain(0, i)
-            deliver(0, i)
-        for n in (1, 2, 3):
-            relay(*steps[n])
-            chain(1, n - 1)
-            deliver(1, n - 1)
-        chain(1, 3)
-        deliver(1, 3)
-
-    for step in steps:
-        settle(*step)
+            block(0, i)
+        relay(*steps[1])
+        settle(*steps[0])
+        block(1, 0)
+        relay(*steps[2])
+        settle(*steps[1])
+        block(1, 1)
+        block(1, 2)
+        relay(*steps[3])
+        settle(*steps[2])
+        block(1, 3)
+        settle(*steps[3])
+
     for (m, i, e), cp in final.items():
         if i < 3:
             cp.wait_recv()
             cp.wait_send()
         else:
             cp.wait()
-    for cp in sends:
+    for cp in sends + list(win.values()):
         cp.wait_send()
 
     @pl.when(holds)
@@ -469,7 +497,7 @@
 
     @pl.when(lacks)
     def _():
-        for cp in wcross + list(rout.values()):
+        for cp in list(wcross.values()) + list(rout.values()):
             cp.wait_send()
         for h in range(2):
             ret[h].wait_recv()
@@ -522,8 +550,8 @@
             dma((MB,)), dma((MB,)),
             dma((MB, 2, 3)), dma((MB, 2, 3)),
             dma((MB, 2, 3, 2)), dma((MB, 2, 3, 2)),
-            dma((2,)), dma((2,)),
-            dma((2, 2, 2)), dma((2, 2, 2)),
+            dma((8,)), dma((8,)),
+            dma((8, 2)), dma((8, 2)),
             dma((MB, 7)), dma((MB, 7)),
             dma((8,)), dma((8,)),
             dma((MB, 3, 2)), dma((MB, 3, 2)),

time: 119 us -> 102 us (0.86)
  Pallas kernels: 112 us -> 94.2 us
    pallas_call x1, Pallas kernels: 112 us -> 94.2 us  [on_device(): pl.pallas_call(kernel, name='backward', out_shape=(jax.ShapeDtypeStruct((...]
where the time goes in v5:
time: 102 us; the launch traced here: 100 us
  Pallas kernels  94.2 us (92%)
  other arithmetic  5.5 us (5%)
    pallas_call x1, Pallas kernels, on_device(): pl.pallas_call(kernel, name='backward', out_shape=(jax.ShapeDtypeStruct((...  94.2 us
    broadcast_in_dim x2, other arithmetic, on_device(): return (grads[None], (weight.astype(F32) * factor)[None])  5.5 us

profile of v5, /device:TPU:4, one launch (start us, length us, event | category | flops | bytes accessed | tf_op | source)
XLA Modules:
  0.0 100.4 jit_solution(13529413299954329059)
XLA Ops:
  0.6 0.0 copy-start
  0.6 94.2 %backward.1 = (bf16[2,128,4096]{2,1,0:T(8,128)(2,1)}, bf16[512,512]{1,0:T(8,128)(2,1)}) custom-call(bf16[1,2,128,8192]{3,2,1,0:T(8,128)(2,1)} %x_hbm.1, bf16[1,2,128,512]{3,2,1,0:T(8,128)(2,1)} %c_hbm.1, bf16[1,512,512]{2,1,0:T(8,128)(2,1)} %w_hbm.1, f32[1,8192]{1,0:T(1,128)} %gain.1, s32[1,2]{1,0:T(1,128)} %bitcast.5), custom_call_target="tpu_custom_call" | custom-call | tf_op jit(solution)/shard_map/backward/pallas_call | solution.py:514
  94.9 0.0 copy-done
  94.9 0.0 copy-start.1
  94.9 4.4 %add_bitcast_fusion = f32[1,2,128,4096]{3,2,1,0:T(8,128)} fusion(bf16[2,128,4096]{2,1,0:T(8,128)(2,1)} %get-tuple-element.4, bf16[2,128,4096]{2,1,0:T(8,128)(2,1)S(1)} %copy-done), kind=kLoop, calls=%fused_computation | loop fusion | flops 3145728 | bytes 8388608 | tf_op jit(solution)/shard_map/broadcast_in_dim | solution.py:569
  99.3 0.0 copy-done.1
  99.3 1.1 %multiply_bitcast_fusion = f32[1,512,512]{2,1,0:T(8,128)} fusion(bf16[512,512]{1,0:T(8,128)(2,1)S(1)} %copy-done.1), kind=kLoop, calls=%fused_computation.1 | loop fusion | flops 524288 | bytes 1572864 | tf_op jit(solution)/shard_map/broadcast_in_dim | solution.py:569
Async XLA Ops:
  0.6 94.2 %copy-start = (bf16[2,128,4096]{2,1,0:T(8,128)(2,1)S(1)}, bf16[2,128,4096]{2,1,0:T(8,128)(2,1)}, u32[]{:S(2)}) copy-start(bf16[2,128,4096]{2,1,0:T(8,128)(2,1)} %param.11) | copy-start | bytes 6291460
  94.9 4.4 %copy-start.1 = (bf16[512,512]{1,0:T(8,128)(2,1)S(1)}, bf16[512,512]{1,0:T(8,128)(2,1)}, u32[]{:S(2)}) copy-start(bf16[512,512]{1,0:T(8,128)(2,1)} %get-tuple-element.5) | copy-start | bytes 1572868

commit v6 on v5

--- a/solution.py
+++ b/solution.py
@@ -36,8 +36,8 @@
 def kernel(
     x_hbm, c_hbm, w_hbm, gain, keep,
     s_out, w_out,
-    cot, rowx, cg, wg, xg, scaled, normed, acc, invb, coefb, squares, stat, wp, rsi, opp, rso, rsr, fb, sb, ci,
-    loc, qs, qr, zs, zr, cs, cr, xs, xr, ps, pr, ws, wr, ts, tr, hs, hr, as_, ar, os_, or_, rs, rr, bs, br,
+    cot, rowx, cg, wg, xg, scaled, normed, acc, invb, coefb, squares, stat, wp, rsi, opp, rso, rsr, fb, sb, ci, via,
+    loc, qs, qr, zs, zr, cs, cr, xs, xr, ps, pr, ws, wr, ts, tr, hs, hr, vs, vr, as_, ar, os_, or_, rs, rr, bs, br,
 ):
     sec = lax.axis_index("section")
     dp = lax.axis_index("dp")
@@ -95,6 +95,7 @@
     barrier = pltpu.get_barrier_semaphore()
     peers = [at(x, (y + k) % 4, (t + e) % 2) for k, e in stat_peers]
     peers += [inner, outer, ((sec + 1) % 4, dp, t), ((sec + 3) % 4, dp, t)]
+    peers += [((sec + 2) % 4, dp, 1 - t)]
     for dev in peers:
         pl.semaphore_signal(barrier, inc=1, device_id=dev, device_id_type=MESH)
     own_c.wait()
@@ -248,7 +249,6 @@
     weight_step(5)
     weight_step(6)
     weight_step(7)
-    send_x(1, 1)
 
     for cp in sums:
         cp.wait_recv()
@@ -339,6 +339,21 @@
                 else:
                     final[m, i, e] = pltpu.make_async_copy(src, spot, loc.at[2 + 2 * m + e])
 
+    hops = {}
+    for m in range(MB):
+        yb = (y + spots[3]) % 4
+        hops[m, 0] = remote(sb.at[m, yb], via.at[m, 0], vs.at[m, 0], vr.at[m, 0], (0, dp, 1 - t))
+        hops[m, 1] = remote(via.at[m, 0], via.at[m, 1], vs.at[m, 1], vr.at[m, 1], (3, dp, t))
+        hops[m, 2] = remote(
+            via.at[m, 1], ci.at[m * 4 + 3], vs.at[m, 2], hr.at[m * 4 + 3], (1, dp, 1 - t)
+        )
+
+    def forward(m, n):
+        @pl.when(sec == (0 if n == 0 else 3))
+        def _():
+            hops[m, n].wait_recv()
+            hops[m, n + 1].start()
+
     def chain(m, i):
         yb = (y + spots[i]) % 4
         cp = chained[m, i]
@@ -365,9 +380,19 @@
         def _():
             put(False)
 
-        @pl.when(sec > 0)
-        def _():
-            cp.start()
+        if i == 3:
+            @pl.when(sec % 2 == 1)
+            def _():
+                cp.start()
+
+            @pl.when(sec == 2)
+            def _():
+                hops[m, 0].start()
+
+        else:
+            @pl.when(sec > 0)
+            def _():
+                cp.start()
 
     def deliver(m, i):
         for e in range(2):
@@ -430,52 +455,66 @@
     inputs(0, 1)
     dots(0)
     arrivals = share(0)
+    send_x(1, 1)
     cotangent(1)
-    multiply(1)
-    coefficients(0, arrivals)
-
-    @pl.when(sec >= 2)
-    def _():
-        for i in blocks:
-            chain(0, i)
-
     inputs(1, 0)
     weights(0)
+    coefficients(0, arrivals)
+
+    @pl.when(sec >= 2)
+    def _():
+        for i in (3, 0, 1, 2):
+            chain(0, i)
+
+    multiply(1)
     inputs(1, 1)
     dots(1)
     arrivals = share(1)
     weights(1)
     relay(*steps[0])
+
+    @pl.when(sec >= 2)
+    def _():
+        for i in blocks:
+            deliver(0, i)
+
+    @pl.when(sec < 2)
+    def _():
+        forward(0, 0)
+        block(0, 0)
+        block(0, 1)
+
     coefficients(1, arrivals)
 
     @pl.when(sec >= 2)
     def _():
-        for i in blocks:
+        for i in (3, 0, 1, 2):
             chain(1, i)
-        for m in range(MB):
-            for i in blocks:
-                deliver(m, i)
+            deliver(1, i)
+        forward(0, 1)
         relay(*steps[1])
         settle(*steps[0])
         relay(*steps[2])
         settle(*steps[1])
+        forward(1, 1)
         relay(*steps[3])
         settle(*steps[2])
         settle(*steps[3])
 
     @pl.when(sec < 2)
     def _():
-        for i in blocks:
-            block(0, i)
         relay(*steps[1])
+        block(0, 2)
+        forward(1, 0)
         settle(*steps[0])
-        block(1, 0)
+        block(0, 3)
         relay(*steps[2])
         settle(*steps[1])
+        block(1, 0)
         block(1, 1)
-        block(1, 2)
         relay(*steps[3])
         settle(*steps[2])
+        block(1, 2)
         block(1, 3)
         settle(*steps[3])
 
@@ -504,8 +543,26 @@
 
     @pl.when(sec > 0)
     def _():
-        for cp in chained.values():
-            cp.wait_send()
+        for (m, i), cp in chained.items():
+            if i < 3:
+                cp.wait_send()
+
+    for n, sender in enumerate((2, 0, 3)):
+
+        @pl.when(sec == sender)
+        def _():
+            for m in range(MB):
+                hops[m, n].wait_send()
+
+    @pl.when(sec % 2 == 1)
+    def _():
+        for m in range(MB):
+            chained[m, 3].wait_send()
+
+
+def finish(factor, top, sums, weight, grads, scaled):
+    grads[...] = top[...].astype(F32) + sums[...].astype(F32)
+    scaled[...] = weight[...].astype(F32) * factor
 
 
 def on_device(layer_inputs, value_cotangent, value_weight, norm_gain, skip_keep, top_grad):
@@ -545,6 +602,7 @@
             pltpu.VMEM((4, 256, HALF), BF16),
             pltpu.VMEM((MB, 4, ROWS, SUB), BF16),
             pltpu.VMEM((8, ROWS, SUB), BF16),
+            pltpu.VMEM((MB, 2, ROWS, SUB), BF16),
             dma((9,)),
             dma((7,)), dma((7,)),
             dma((MB,)), dma((MB,)),
@@ -554,6 +612,7 @@
             dma((8, 2)), dma((8, 2)),
             dma((MB, 7)), dma((MB, 7)),
             dma((8,)), dma((8,)),
+            dma((MB, 3)), dma((MB, 2)),
             dma((MB, 3, 2)), dma((MB, 3, 2)),
             dma((4,)), dma((4,)),
             dma((4,)), dma((4,)),
@@ -565,8 +624,26 @@
     )(layer_inputs, value_cotangent, value_weight, norm_gain, skip_keep.reshape(1, MB))
     total_rows = MB * ROWS * lax.axis_size("dp")
     factor = float(total_rows) ** (-0.5)
-    grads = top_grad.astype(F32) + sums.astype(F32)
-    return grads[None], (weight.astype(F32) * factor)[None]
+    rows, cols = MB * ROWS // 4, HALF // 4
+    grads, scaled = pl.pallas_call(
+        functools.partial(finish, factor),
+        name="finish",
+        out_shape=(
+            jax.ShapeDtypeStruct((MB * ROWS, 4096), F32),
+            jax.ShapeDtypeStruct((HALF, HALF), F32),
+        ),
+        grid=(4,),
+        in_specs=[
+            pl.BlockSpec((rows, 4096), lambda i: (i, 0)),
+            pl.BlockSpec((rows, 4096), lambda i: (i, 0)),
+            pl.BlockSpec((cols, HALF), lambda i: (i, 0)),
+        ],
+        out_specs=(
+            pl.BlockSpec((rows, 4096), lambda i: (i, 0)),
+            pl.BlockSpec((cols, HALF), lambda i: (i, 0)),
+        ),
+    )(top_grad.reshape(MB * ROWS, 4096), sums.reshape(MB * ROWS, 4096), weight)
+    return grads.reshape(1, MB, ROWS, 4096), scaled[None]
 
 
 def solution(mesh):

time: 102 us -> 97.5 us (0.956)
  other arithmetic: 5.5 us -> 0 us
  Pallas kernels: 94.2 us -> 95.5 us
    broadcast_in_dim x2 -> x0, other arithmetic: 5.5 us -> none  [on_device(): return (grads[None], (weight.astype(F32) * factor)[None])]
    pallas_call x0 -> x1, Pallas kernels: none -> 5.12 us  [on_device(): pl.pallas_call(functools.partial(finish, factor), name='finish', out_shap...]
    pallas_call x1, Pallas kernels: 94.2 us -> 90.4 us  [on_device(): pl.pallas_call(kernel, name='backward', out_shape=(jax.ShapeDtypeStruct((...]
where the time goes in v6:
time: 97.5 us; the launch traced here: 96.1 us
  Pallas kernels  95.5 us (98%)
    pallas_call x1, Pallas kernels, on_device(): pl.pallas_call(kernel, name='backward', out_shape=(jax.ShapeDtypeStruct((...  90.4 us
    pallas_call x1, Pallas kernels, on_device(): pl.pallas_call(functools.partial(finish, factor), name='finish', out_shap...  5.12 us

profile of v6, /device:TPU:4, one launch (start us, length us, event | category | flops | bytes accessed | tf_op | source)
XLA Modules:
  0.0 96.1 jit_solution(427790636711312765)
XLA Ops:
  0.6 90.4 %backward.1 = (bf16[2,128,4096]{2,1,0:T(8,128)(2,1)}, bf16[512,512]{1,0:T(8,128)(2,1)}) custom-call(bf16[1,2,128,8192]{3,2,1,0:T(8,128)(2,1)} %x_hbm.1, bf16[1,2,128,512]{3,2,1,0:T(8,128)(2,1)} %c_hbm.1, bf16[1,512,512]{2,1,0:T(8,128)(2,1)} %w_hbm.1, f32[1,8192]{1,0:T(1,128)} %gain.1, s32[1,2]{1,0:T(1,128)} %bitcast.7), custom_call_target="tpu_custom_call" | custom-call | tf_op jit(solution)/shard_map/backward/pallas_call | solution.py:571
  91.0 5.1 %finish.1 = (f32[256,4096]{1,0:T(8,128)}, f32[512,512]{1,0:T(8,128)}) custom-call(bf16[256,4096]{1,0:T(8,128)(2,1)} %bitcast.5, bf16[256,4096]{1,0:T(8,128)(2,1)} %bitcast.6, bf16[512,512]{1,0:T(8,128)(2,1)} %get-tuple-element.7.weight), custom_call_target="tpu_custom_call" | custom-call | tf_op jit(solution)/shard_map/finish/pallas_call | solution.py:628

commit v7 on v6

--- a/solution.py
+++ b/solution.py
@@ -264,21 +264,21 @@
             for i in range(3):
                 wait_cot((m, half, i))
 
-    def multiply(m):
+    def multiply(m, h):
         if m == 0:
-            for cp in win.values():
-                cp.wait_recv()
-
-        def tile(i, carry):
-            rows = pl.ds(pl.multiple_of((i % 2) * 256, 256), 256)
-            cols = pl.ds(pl.multiple_of(i * 256, 256), 256)
-            ng = nt(cg[m, 0].reshape(HALF, HALF), wg[i // 2, 0, rows, :])
-            ng += nt(cg[m, 1].reshape(HALF, HALF), wg[i // 2, 1, rows, :])
-            start = pl.multiple_of(feature(i // 2, y) + (i % 2) * 256, 256)
+            for n in (0, 1, 4, 5):
+                win[n + 2 * h].wait_recv()
+
+        def tile(e, carry):
+            rows = pl.ds(h * 256, 256)
+            cols = pl.ds(pl.multiple_of(e * HALF + h * 256, 256), 256)
+            ng = nt(cg[m, 0].reshape(HALF, HALF), wg[e, 0, rows, :])
+            ng += nt(cg[m, 1].reshape(HALF, HALF), wg[e, 1, rows, :])
+            start = pl.multiple_of(feature(e, y) + h * 256, 256)
             scaled[m, :, cols] = ng * gain[0:1, pl.ds(start, 256)]
             return carry
 
-        lax.fori_loop(0, 4, tile, 0)
+        lax.fori_loop(0, 2, tile, 0)
 
     def inputs(m, h):
         if h == 0:
@@ -299,16 +299,18 @@
 
         lax.fori_loop(0, 4, tile, 0)
 
-    def dots(m):
-        acc[...] = jnp.zeros_like(acc)
+    def dots(m, h):
+        if h == 0:
+            acc[...] = jnp.zeros_like(acc)
 
         def tile(i, carry):
-            cols = pl.ds(pl.multiple_of(i * 128, 128), 128)
+            at_col = pl.multiple_of((i // 2) * HALF + h * 256 + (i % 2) * 128, 128)
+            cols = pl.ds(at_col, 128)
             xf = xg[m, :, :, cols].reshape(HALF, 128).astype(F32)
             acc[...] += xf * scaled[m, :, cols]
             return carry
 
-        lax.fori_loop(0, 8, tile, 0)
+        lax.fori_loop(0, 4, tile, 0)
 
     def share(m):
         stat[m, me] = exact(ones, acc[...], ((1,), (1,)))
@@ -322,7 +324,7 @@
         inv = invb[m].reshape(HALF, 128)
         coefb[m] = (inv * inv * inv * wide).reshape(4, ROWS, 128)
 
-    below = (sec - 1, dp, t)
+    below = ((sec + 3) % 4, dp, t)
     chained = {}
     final = {}
     spots = (2, 1, 3, 0)
@@ -450,10 +452,12 @@
         deliver(m, i)
 
     cotangent(0)
-    multiply(0)
+    multiply(0, 0)
     inputs(0, 0)
+    dots(0, 0)
     inputs(0, 1)
-    dots(0)
+    multiply(0, 1)
+    dots(0, 1)
     arrivals = share(0)
     send_x(1, 1)
     cotangent(1)
@@ -466,9 +470,11 @@
         for i in (3, 0, 1, 2):
             chain(0, i)
 
-    multiply(1)
+    multiply(1, 0)
+    multiply(1, 1)
+    dots(1, 0)
     inputs(1, 1)
-    dots(1)
+    dots(1, 1)
     arrivals = share(1)
     weights(1)
     relay(*steps[0])

time: 97.5 us -> 97.3 us (level)
  no operation moved by 1% of the time
where the time goes in v7:
time: 97.3 us; the launch traced here: 95.4 us
  Pallas kernels  94.8 us (97%)
    pallas_call x1, Pallas kernels, on_device(): pl.pallas_call(kernel, name='backward', out_shape=(jax.ShapeDtypeStruct((...  89.6 us
    pallas_call x1, Pallas kernels, on_device(): pl.pallas_call(functools.partial(finish, factor), name='finish', out_shap...  5.12 us

profile of v7, /device:TPU:4, one launch (start us, length us, event | category | flops | bytes accessed | tf_op | source)
XLA Modules:
  0.0 95.4 jit_solution(11872473902981078717)
XLA Ops:
  0.6 89.6 %backward.1 = (bf16[2,128,4096]{2,1,0:T(8,128)(2,1)}, bf16[512,512]{1,0:T(8,128)(2,1)}) custom-call(bf16[1,2,128,8192]{3,2,1,0:T(8,128)(2,1)} %x_hbm.1, bf16[1,2,128,512]{3,2,1,0:T(8,128)(2,1)} %c_hbm.1, bf16[1,512,512]{2,1,0:T(8,128)(2,1)} %w_hbm.1, f32[1,8192]{1,0:T(1,128)} %gain.1, s32[1,2]{1,0:T(1,128)} %bitcast.7), custom_call_target="tpu_custom_call" | custom-call | tf_op jit(solution)/shard_map/backward/pallas_call | solution.py:577
  90.3 5.1 %finish.1 = (f32[256,4096]{1,0:T(8,128)}, f32[512,512]{1,0:T(8,128)}) custom-call(bf16[256,4096]{1,0:T(8,128)(2,1)} %bitcast.5, bf16[256,4096]{1,0:T(8,128)(2,1)} %bitcast.6, bf16[512,512]{1,0:T(8,128)(2,1)} %get-tuple-element.7.weight), custom_call_target="tpu_custom_call" | custom-call | tf_op jit(solution)/shard_map/finish/pallas_call | solution.py:634

commit v8 on v7

--- a/solution.py
+++ b/solution.py
@@ -630,7 +630,7 @@
     )(layer_inputs, value_cotangent, value_weight, norm_gain, skip_keep.reshape(1, MB))
     total_rows = MB * ROWS * lax.axis_size("dp")
     factor = float(total_rows) ** (-0.5)
-    rows, cols = MB * ROWS // 4, HALF // 4
+    rows, cols = MB * ROWS // 2, HALF // 2
     grads, scaled = pl.pallas_call(
         functools.partial(finish, factor),
         name="finish",
@@ -638,7 +638,7 @@
             jax.ShapeDtypeStruct((MB * ROWS, 4096), F32),
             jax.ShapeDtypeStruct((HALF, HALF), F32),
         ),
-        grid=(4,),
+        grid=(2,),
         in_specs=[
             pl.BlockSpec((rows, 4096), lambda i: (i, 0)),
             pl.BlockSpec((rows, 4096), lambda i: (i, 0)),

time: 97.3 us -> 96.2 us (0.989)
  Pallas kernels: 94.8 us -> 93.8 us
where the time goes in v8:
time: 96.2 us; the launch traced here: 94.4 us
  Pallas kernels  93.8 us (98%)
    pallas_call x1, Pallas kernels, on_device(): pl.pallas_call(kernel, name='backward', out_shape=(jax.ShapeDtypeStruct((...  89.6 us
    pallas_call x1, Pallas kernels, on_device(): pl.pallas_call(functools.partial(finish, factor), name='finish', out_shap...  4.15 us

profile of v8, /device:TPU:4, one launch (start us, length us, event | category | flops | bytes accessed | tf_op | source)
XLA Modules:
  0.0 94.4 jit_solution(12570762687321717138)
XLA Ops:
  0.6 89.6 %backward.1 = (bf16[2,128,4096]{2,1,0:T(8,128)(2,1)}, bf16[512,512]{1,0:T(8,128)(2,1)}) custom-call(bf16[1,2,128,8192]{3,2,1,0:T(8,128)(2,1)} %x_hbm.1, bf16[1,2,128,512]{3,2,1,0:T(8,128)(2,1)} %c_hbm.1, bf16[1,512,512]{2,1,0:T(8,128)(2,1)} %w_hbm.1, f32[1,8192]{1,0:T(1,128)} %gain.1, s32[1,2]{1,0:T(1,128)} %bitcast.7), custom_call_target="tpu_custom_call" | custom-call | tf_op jit(solution)/shard_map/backward/pallas_call | solution.py:577
  90.3 4.2 %finish.1 = (f32[256,4096]{1,0:T(8,128)}, f32[512,512]{1,0:T(8,128)}) custom-call(bf16[256,4096]{1,0:T(8,128)(2,1)} %bitcast.5, bf16[256,4096]{1,0:T(8,128)(2,1)} %bitcast.6, bf16[512,512]{1,0:T(8,128)(2,1)} %get-tuple-element.7.weight), custom_call_target="tpu_custom_call" | custom-call | tf_op jit(solution)/shard_map/finish/pallas_call | solution.py:634
